TPU v7x, 32 devices: a whole 2x2x4 slice. The times are simulated.
32 devices in a mesh: runs: 2 (over y), curve: 4 (over z), sub: 4 (over x, core).
Axes of the slice: x: 2, y: 2, z: 4, core: 2. Of those that a mesh axis runs over, the one named last changes fastest.
Arguments:
- positions: float32 [3, 16384, 128], P(None, ('runs', 'curve', 'sub')), parts along dimension 1, may hold values from -1 to 1
- strengths: float32 [3, 16384, 128], P(None, ('runs', 'curve', 'sub')), parts along dimension 1, may hold values from -6 to 6
- counts: int32 [16384], P(('runs', 'curve', 'sub')), parts along dimension 0, may hold values from 1 to 128
- frequencies: float32 [3, 128], replicated, may hold values from -3 to 3
- phases: float32 [128], replicated, may hold values from -3.140625 to 3.140625
- charge_dirs: float32 [3, 128], replicated, may hold values from -0.3125 to 0.3125
- velocity_dirs: float32 [3, 128], replicated, may hold values from -0.5 to 0.5
- up_maps: float32 [8, 128, 128], replicated, may hold values from -0.1875 to 0.1875
- down_maps: float32 [8, 128, 128], replicated, may hold values from -0.5 to 0.5
- far_maps: float32 [16, 128, 128], replicated, may hold values from -0.09375 to 0.09375
- coarse_maps: float32 [16, 128, 128], replicated, may hold values from -0.046875 to 0.046875
- send_boxes: int32 [512, 8], P(('runs', 'curve', 'sub')), parts along dimension 0, may hold values from 0 to 511
- far_source: int32 [16384, 32], P(('runs', 'curve', 'sub')), parts along dimension 0, may hold values from 0 to 1151, as said below
- far_class: int32 [16384, 32], P(('runs', 'curve', 'sub')), parts along dimension 0, may hold values from 0 to 15
- near_source: int32 [16384, 2], P(('runs', 'curve', 'sub')), parts along dimension 0, may hold values from 0 to 519, as said below
- coarse_class: int32 [256, 128], P(('runs', 'curve', 'sub')), parts along dimension 0, may hold values from 0 to 15
Outputs:
- velocity: float32 [3, 16384, 128], P(None, ('runs', 'curve', 'sub')), parts along dimension 1
There are 2 independent parts, one for each index of `runs`. A program takes and returns all parts, laid end to end along the dimension named above; an argument that names none is the same for every part. Nothing has to cross between parts.
Inputs may be any that keep to these rules, and one draw needn't show every extreme that they name: `send_boxes`: local leaf box numbers of the sending device; any box may be sent several times or not at all. `far_source`: every received row 1024 to 1151 of a device's source table is named by exactly one entry of that device's boxes; all other entries name rows below 1024, the device's own boxes and the 256 boxes on each side along the curve. `near_source`: entry l of box r of a device is 4 + r + o with o a nonzero offset of at most 4 in size; entries may repeat.
All inputs are finite; a program needn't handle non-finite values.
Results may differ from a plain program's by a relative error of at most 0.0003.
Values sent between devices are 32-bit elements; how exact they have to be, the bound alone decides.
A program may use at most 64 MiB of HBM per device.

v0:
```python
import math

import jax
import jax.numpy as jnp
from jax import lax
from jax.sharding import PartitionSpec as P

HW = 4


highest = lax.Precision.HIGHEST
smoothing_sq = 0.25
inverse_four_pi = 0.25 / math.pi
leaf_group = 64
near_group = 32


def padded(cells, sides, width):
    for axis, dim in sides:
        count = lax.axis_size(axis)
        ends = count - 1
        head = lax.slice_in_dim(cells, 0, width, axis=dim)
        tail = lax.slice_in_dim(cells, cells.shape[dim] - width, cells.shape[dim], axis=dim)
        cells = jnp.concatenate(
            [
                lax.ppermute(tail, axis, [(i, (i + 1) % count) for i in range(ends)]),
                cells,
                lax.ppermute(head, axis, [((i + 1) % count, i) for i in range(ends)]),
            ],
            axis=dim,
        )
    return cells


def features(coords, frequencies, phases):
    angles = (
        jnp.einsum("ik,ibp->bkp", frequencies, coords, precision=highest) + phases[None, :, None]
    )
    return jnp.cos(angles)


def moments_of(coords, charged, frequencies, phases, charge_dirs):
    basis = features(coords, frequencies, phases)
    weights = jnp.einsum("ik,ibp->bkp", charge_dirs, charged, precision=highest)
    return jnp.sum(basis * weights, axis=2)


def velocity_of(coords, expansion, frequencies, phases, velocity_dirs):
    basis = features(coords, frequencies, phases)
    scaled = expansion[:, :, None] * basis
    return jnp.einsum("ik,bkp->ibp", velocity_dirs, scaled, precision=highest)


def upward(maps, child):
    grouped_child = child.reshape(-1, 8, child.shape[-1])
    return jnp.einsum("jkl,qjl->qk", maps, grouped_child, precision=highest)


def downward(maps, parent):
    return jnp.einsum("jkl,ql->qjk", maps, parent, precision=highest).reshape(-1, parent.shape[-1])


def translate(maps, classes, sources):
    onehot = (
        classes[:, :, None] == jnp.arange(maps.shape[0], dtype=jnp.int32)[None, None, :]
    ).astype(jnp.float32)
    summed = jnp.einsum("bln,blk->nbk", onehot, sources, precision=highest)
    return jnp.einsum("nkl,nbl->bk", maps, summed, precision=highest)


def coarse_translate(maps, classes, sources):
    onehot = (
        classes[:, :, None] == jnp.arange(maps.shape[0], dtype=jnp.int32)[None, None, :]
    ).astype(jnp.float32)
    summed = jnp.einsum("ten,ek->ntk", onehot, sources, precision=highest)
    return jnp.einsum("nkl,ntl->tk", maps, summed, precision=highest)


def cross_sum(targets, sources, source_strength):
    diff = targets[:, :, :, None] - sources[:, :, None, :]
    dist = jnp.sum(diff * diff, axis=0) + smoothing_sq
    kernel = inverse_four_pi / (dist * jnp.sqrt(dist))
    alpha = source_strength[:, :, None, :]
    first = alpha[1] * diff[2] - alpha[2] * diff[1]
    second = alpha[2] * diff[0] - alpha[0] * diff[2]
    third = alpha[0] * diff[1] - alpha[1] * diff[0]
    return jnp.stack(
        [
            jnp.sum(first * kernel, axis=-1),
            jnp.sum(second * kernel, axis=-1),
            jnp.sum(third * kernel, axis=-1),
        ]
    )


def near_field(ext_coords, ext_charged, near_rows, margin):
    box_total = near_rows.shape[0]
    own_rows = margin + jnp.arange(box_total, dtype=jnp.int32)
    listed = jnp.concatenate([own_rows[:, None], near_rows], axis=1)

    def block(start_box):
        chosen = lax.dynamic_slice_in_dim(listed, start_box, near_group, 0)
        targets = lax.dynamic_slice_in_dim(ext_coords, start_box + margin, near_group, 1)
        total = jnp.zeros(targets.shape, jnp.float32)
        for column in range(listed.shape[1]):
            rows_here = chosen[:, column]
            src_coords = jnp.take(ext_coords, rows_here, axis=1)
            src_charged = jnp.take(ext_charged, rows_here, axis=1)
            total = total + cross_sum(targets, src_coords, src_charged)
        return total

    starts = jnp.arange(0, box_total, near_group, dtype=jnp.int32)
    pieces = lax.map(block, starts)
    return jnp.transpose(pieces, (1, 0, 2, 3)).reshape(3, box_total, -1)


def leaf_blocks(coords):
    return jnp.transpose(coords.reshape(3, -1, leaf_group, coords.shape[-1]), (1, 0, 2, 3))


def shards(
    positions,
    strengths,
    counts,
    frequencies,
    phases,
    charge_dirs,
    velocity_dirs,
    up_maps,
    down_maps,
    far_maps,
    coarse_maps,
    send_boxes,
    far_source,
    far_class,
    near_source,
    coarse_class,
):
    box_count = positions.shape[1]
    slot_count = positions.shape[2]
    coeffs = frequencies.shape[1]
    moment_reach = box_count // 2
    slot_index = jnp.arange(slot_count, dtype=jnp.int32)
    occupied = (slot_index[None, :] < counts[:, None]).astype(jnp.float32)
    charged = strengths * occupied[None]
    packed = jnp.concatenate([positions, charged], axis=0)
    extended = padded(packed, ((("curve", "sub"), 1),), HW)
    blocks_pos = leaf_blocks(positions)
    blocks_charge = leaf_blocks(charged)
    leaf_moments = lax.map(
        lambda blocks_in: moments_of(blocks_in[0], blocks_in[1], frequencies, phases, charge_dirs),
        (blocks_pos, blocks_charge),
    ).reshape(box_count, coeffs)
    nearby_moments = padded(leaf_moments, ((("curve", "sub"), 0),), moment_reach)
    parcel = leaf_moments[send_boxes]
    received = lax.all_to_all(parcel, ("curve", "sub"), split_axis=0, concat_axis=0, tiled=True)
    top_moments = upward(up_maps, upward(up_maps, leaf_moments))
    coarse_moments = lax.all_gather(top_moments, ("curve", "sub"), axis=0, tiled=True)
    coarse_locals = coarse_translate(coarse_maps, coarse_class, coarse_moments)
    leaf_down = downward(down_maps, downward(down_maps, coarse_locals))
    lookup = jnp.concatenate([nearby_moments, received.reshape(-1, coeffs)], axis=0)
    leaf_locals = leaf_down + translate(far_maps, far_class, lookup[far_source])
    far_velocity = lax.map(
        lambda blocks_in: velocity_of(
            blocks_in[0], blocks_in[1], frequencies, phases, velocity_dirs
        ),
        (blocks_pos, leaf_locals.reshape(-1, leaf_group, coeffs)),
    )
    far_velocity = jnp.transpose(far_velocity, (1, 0, 2, 3)).reshape(3, box_count, slot_count)
    near_velocity = near_field(extended[:3], extended[3:], near_source, HW)
    return (far_velocity + near_velocity) * occupied[None]


def solution(mesh):
    return jax.shard_map(
        shards,
        mesh=mesh,
        in_specs=(
            P(None, ("runs", "curve", "sub"), None),
            P(None, ("runs", "curve", "sub"), None),
            P(("runs", "curve", "sub")),
            P(),
            P(),
            P(),
            P(),
            P(),
            P(),
            P(),
            P(),
            P(("runs", "curve", "sub"), None),
            P(("runs", "curve", "sub"), None),
            P(("runs", "curve", "sub"), None),
            P(("runs", "curve", "sub"), None),
            P(("runs", "curve", "sub"), None),
        ),
        out_specs=P(None, ("runs", "curve", "sub"), None),
        check_vma=False,
    )
```

profile of v0, /device:TPU:0, one launch (start us, length us, event | category | flops | bytes accessed | tf_op | source)
XLA Modules:
  0.0 1037.8 jit_solution(12608727492875365126)
XLA Ops:
  5.3 223.6 %while.32 = (s32[]{:T(128)}, f32[8,64,128]{2,1,0:T(8,128)S(1)}, f32[8,3,64,128]{3,1,2,0:T(4,128)}, f32[3,128]{1,0:T(4,128)S(1)}, f32[128]{0:T(128)S(1)}, /*index...) while((s32[]{:T(128)}, f32[8,64,128]{2,1,0:T(8,128)S(1)}, f32[8,3,64,128]{3,1,2,0:T(4,128)}, ...), condition=%wide.region_2.3_spmd, body=%wide.region_0.2_spmd.sunk | while | flops 78635008 | bytes 8753753 | solution.py:150
  12.9 20.3 %multiply_reduce_fusion.18 = f32[64,128]{1,0:T(8,128)S(1)} fusion(f32[64,128,128]{2,1,0:T(8,128)S(1)} %fusion.87, f32[128]{0:T(128)S(1)} %get-tuple-element.543, f32[8,3,64,128]{3,1,2,0:T(4,128)} %get-tuple-element.544, s32[]{:T(128)} %get-tuple-element.531, f32[3,128]{1,0:T(4,128)S(1)} %get-tuple-element.545), kind=kOutput, calls=%fused_computation.8.clone.1 | convolution fusion | flops 40886272 | bytes 4360704 | tf_op jit(solution)/shard_map/while/body/eval_jaxpr/ik,ibp->bkp/dot_general | solution.py:44
  40.9 20.3 %multiply_reduce_fusion.18 = f32[64,128]{1,0:T(8,128)S(1)} fusion(f32[64,128,128]{2,1,0:T(8,128)S(1)} %fusion.87, f32[128]{0:T(128)S(1)} %get-tuple-element.543, f32[8,3,64,128]{3,1,2,0:T(4,128)} %get-tuple-element.544, s32[]{:T(128)} %get-tuple-element.531, f32[3,128]{1,0:T(4,128)S(1)} %get-tuple-element.545), kind=kOutput, calls=%fused_computation.8.clone.1 | convolution fusion | flops 40886272 | bytes 4360704 | tf_op jit(solution)/shard_map/while/body/eval_jaxpr/ik,ibp->bkp/dot_general | solution.py:44
  68.8 20.3 %multiply_reduce_fusion.18 = f32[64,128]{1,0:T(8,128)S(1)} fusion(f32[64,128,128]{2,1,0:T(8,128)S(1)} %fusion.87, f32[128]{0:T(128)S(1)} %get-tuple-element.543, f32[8,3,64,128]{3,1,2,0:T(4,128)} %get-tuple-element.544, s32[]{:T(128)} %get-tuple-element.531, f32[3,128]{1,0:T(4,128)S(1)} %get-tuple-element.545), kind=kOutput, calls=%fused_computation.8.clone.1 | convolution fusion | flops 40886272 | bytes 4360704 | tf_op jit(solution)/shard_map/while/body/eval_jaxpr/ik,ibp->bkp/dot_general | solution.py:44
  96.8 20.3 %multiply_reduce_fusion.18 = f32[64,128]{1,0:T(8,128)S(1)} fusion(f32[64,128,128]{2,1,0:T(8,128)S(1)} %fusion.87, f32[128]{0:T(128)S(1)} %get-tuple-element.543, f32[8,3,64,128]{3,1,2,0:T(4,128)} %get-tuple-element.544, s32[]{:T(128)} %get-tuple-element.531, f32[3,128]{1,0:T(4,128)S(1)} %get-tuple-element.545), kind=kOutput, calls=%fused_computation.8.clone.1 | convolution fusion | flops 40886272 | bytes 4360704 | tf_op jit(solution)/shard_map/while/body/eval_jaxpr/ik,ibp->bkp/dot_general | solution.py:44
  124.8 20.3 %multiply_reduce_fusion.18 = f32[64,128]{1,0:T(8,128)S(1)} fusion(f32[64,128,128]{2,1,0:T(8,128)S(1)} %fusion.87, f32[128]{0:T(128)S(1)} %get-tuple-element.543, f32[8,3,64,128]{3,1,2,0:T(4,128)} %get-tuple-element.544, s32[]{:T(128)} %get-tuple-element.531, f32[3,128]{1,0:T(4,128)S(1)} %get-tuple-element.545), kind=kOutput, calls=%fused_computation.8.clone.1 | convolution fusion | flops 40886272 | bytes 4360704 | tf_op jit(solution)/shard_map/while/body/eval_jaxpr/ik,ibp->bkp/dot_general | solution.py:44
  152.7 20.3 %multiply_reduce_fusion.18 = f32[64,128]{1,0:T(8,128)S(1)} fusion(f32[64,128,128]{2,1,0:T(8,128)S(1)} %fusion.87, f32[128]{0:T(128)S(1)} %get-tuple-element.543, f32[8,3,64,128]{3,1,2,0:T(4,128)} %get-tuple-element.544, s32[]{:T(128)} %get-tuple-element.531, f32[3,128]{1,0:T(4,128)S(1)} %get-tuple-element.545), kind=kOutput, calls=%fused_computation.8.clone.1 | convolution fusion | flops 40886272 | bytes 4360704 | tf_op jit(solution)/shard_map/while/body/eval_jaxpr/ik,ibp->bkp/dot_general | solution.py:44
  180.7 20.3 %multiply_reduce_fusion.18 = f32[64,128]{1,0:T(8,128)S(1)} fusion(f32[64,128,128]{2,1,0:T(8,128)S(1)} %fusion.87, f32[128]{0:T(128)S(1)} %get-tuple-element.543, f32[8,3,64,128]{3,1,2,0:T(4,128)} %get-tuple-element.544, s32[]{:T(128)} %get-tuple-element.531, f32[3,128]{1,0:T(4,128)S(1)} %get-tuple-element.545), kind=kOutput, calls=%fused_computation.8.clone.1 | convolution fusion | flops 40886272 | bytes 4360704 | tf_op jit(solution)/shard_map/while/body/eval_jaxpr/ik,ibp->bkp/dot_general | solution.py:44
  208.6 20.3 %multiply_reduce_fusion.18 = f32[64,128]{1,0:T(8,128)S(1)} fusion(f32[64,128,128]{2,1,0:T(8,128)S(1)} %fusion.87, f32[128]{0:T(128)S(1)} %get-tuple-element.543, f32[8,3,64,128]{3,1,2,0:T(4,128)} %get-tuple-element.544, s32[]{:T(128)} %get-tuple-element.531, f32[3,128]{1,0:T(4,128)S(1)} %get-tuple-element.545), kind=kOutput, calls=%fused_computation.8.clone.1 | convolution fusion | flops 40886272 | bytes 4360704 | tf_op jit(solution)/shard_map/while/body/eval_jaxpr/ik,ibp->bkp/dot_general | solution.py:44
  235.4 8.6 all-to-all-start
  255.1 23.3 %all_gather.3 = f32[128,128]{1,0:T(8,128)S(1)} all-gather(f32[8,128]{1,0:T(8,128)S(1)} %convolution_bitcast_fusion.2), channel_id=1, replica_groups=mesh['runs'=2,'curve'=4,'sub'=4] {'curve','sub'}, dimensions={0}, use_global_device_ids=true | all-gather | bytes 69632 | tf_op jit(solution)/shard_map/all_gather | solution.py:158
  288.2 460.5 %while.34 = (s32[]{:T(128)}, f32[16,3,32,128]{3,2,1,0:T(8,128)}, s32[16]{0:T(128)S(1)}, s32[512,3]{0,1:T(4,128)S(1)}, f32[3,520,128]{2,0,1:T(4,128)}, /*index=5*...) while((s32[]{:T(128)}, f32[16,3,32,128]{3,2,1,0:T(8,128)}, ...), condition=%wide.region_18.20_spmd, body=%wide.region_5.19_spmd.sunk | while | flops 41033288 | bytes 53001744 | solution.py:113
  328.6 7.6 multiply_reduce_fusion.19
  357.4 7.6 multiply_reduce_fusion.19
  415.0 7.6 multiply_reduce_fusion.19
  472.5 7.6 multiply_reduce_fusion.19
  501.3 7.6 multiply_reduce_fusion.19
  530.1 7.6 multiply_reduce_fusion.19
  558.9 7.6 multiply_reduce_fusion.19
  587.7 7.6 multiply_reduce_fusion.19
  616.4 7.6 multiply_reduce_fusion.19
  731.6 7.6 multiply_reduce_fusion.19
  752.5 54.4 %gather_fusion.7 = f32[16384,128]{1,0:T(8,128)} fusion(f32[1152,128]{1,0:T(8,128)S(1)} %pad_maximum_fusion.1, s32[16384]{0:T(1024)S(1)} %broadcast_clamp_fusion), kind=kCustom, calls=%fused_computation.7 | custom fusion | bytes 16842752 | tf_op jit(solution)/shard_map/gather | solution.py:162
  818.7 216.7 %while.33 = (s32[]{:T(128)}, f32[8,3,64,128]{3,1,2,0:T(4,128)S(1)}, f32[8,64,128]{2,1,0:T(8,128)S(1)}, f32[8,3,64,128]{3,1,2,0:T(4,128)}, f32[3,128]{1,0:T(4,128...) while((s32[]{:T(128)}, f32[8,3,64,128]{3,1,2,0:T(4,128)S(1)}, f32[8,64,128]{2,1,0:T(8,128)S(1)}, ...), condition=%wide.region_4.5_spmd, body=%wide.region_3.4_spmd.sunk | while | flops 77594624 | bytes 8753757 | solution.py:163
  826.5 19.4 %fusion.93 = f32[8,3,64,128]{3,1,2,0:T(4,128)S(1)} fusion(f32[8,3,64,128]{3,1,2,0:T(4,128)S(1)} %get-tuple-element.556, s32[]{:T(128)} %get-tuple-element.555, f32[64,128,128]{2,1,0:T(8,128)S(1)} %fusion.92, f32[128]{0:T(128)S(1)} %get-tuple-element.568, f32[64,128]{1,0:T(8,128)S(1)} %dynamic-slice_bitcast_fusion.2, f32[3,128]{1,0:T(4,128)S(1)} %get-tuple-element.569), kind=kOutput, calls=%fused_computation.27.clone.1 | convolution fusion | flops 39845888 | bytes 4360708 | tf_op jit(solution)/shard_map/while/body/eval_jaxpr/ik,bkp->ibp/dot_general | solution.py:51
  853.6 19.4 %fusion.93 = f32[8,3,64,128]{3,1,2,0:T(4,128)S(1)} fusion(f32[8,3,64,128]{3,1,2,0:T(4,128)S(1)} %get-tuple-element.556, s32[]{:T(128)} %get-tuple-element.555, f32[64,128,128]{2,1,0:T(8,128)S(1)} %fusion.92, f32[128]{0:T(128)S(1)} %get-tuple-element.568, f32[64,128]{1,0:T(8,128)S(1)} %dynamic-slice_bitcast_fusion.2, f32[3,128]{1,0:T(4,128)S(1)} %get-tuple-element.569), kind=kOutput, calls=%fused_computation.27.clone.1 | convolution fusion | flops 39845888 | bytes 4360708 | tf_op jit(solution)/shard_map/while/body/eval_jaxpr/ik,bkp->ibp/dot_general | solution.py:51
  880.7 19.4 %fusion.93 = f32[8,3,64,128]{3,1,2,0:T(4,128)S(1)} fusion(f32[8,3,64,128]{3,1,2,0:T(4,128)S(1)} %get-tuple-element.556, s32[]{:T(128)} %get-tuple-element.555, f32[64,128,128]{2,1,0:T(8,128)S(1)} %fusion.92, f32[128]{0:T(128)S(1)} %get-tuple-element.568, f32[64,128]{1,0:T(8,128)S(1)} %dynamic-slice_bitcast_fusion.2, f32[3,128]{1,0:T(4,128)S(1)} %get-tuple-element.569), kind=kOutput, calls=%fused_computation.27.clone.1 | convolution fusion | flops 39845888 | bytes 4360708 | tf_op jit(solution)/shard_map/while/body/eval_jaxpr/ik,bkp->ibp/dot_general | solution.py:51
  907.7 19.4 %fusion.93 = f32[8,3,64,128]{3,1,2,0:T(4,128)S(1)} fusion(f32[8,3,64,128]{3,1,2,0:T(4,128)S(1)} %get-tuple-element.556, s32[]{:T(128)} %get-tuple-element.555, f32[64,128,128]{2,1,0:T(8,128)S(1)} %fusion.92, f32[128]{0:T(128)S(1)} %get-tuple-element.568, f32[64,128]{1,0:T(8,128)S(1)} %dynamic-slice_bitcast_fusion.2, f32[3,128]{1,0:T(4,128)S(1)} %get-tuple-element.569), kind=kOutput, calls=%fused_computation.27.clone.1 | convolution fusion | flops 39845888 | bytes 4360708 | tf_op jit(solution)/shard_map/while/body/eval_jaxpr/ik,bkp->ibp/dot_general | solution.py:51
  934.8 19.4 %fusion.93 = f32[8,3,64,128]{3,1,2,0:T(4,128)S(1)} fusion(f32[8,3,64,128]{3,1,2,0:T(4,128)S(1)} %get-tuple-element.556, s32[]{:T(128)} %get-tuple-element.555, f32[64,128,128]{2,1,0:T(8,128)S(1)} %fusion.92, f32[128]{0:T(128)S(1)} %get-tuple-element.568, f32[64,128]{1,0:T(8,128)S(1)} %dynamic-slice_bitcast_fusion.2, f32[3,128]{1,0:T(4,128)S(1)} %get-tuple-element.569), kind=kOutput, calls=%fused_computation.27.clone.1 | convolution fusion | flops 39845888 | bytes 4360708 | tf_op jit(solution)/shard_map/while/body/eval_jaxpr/ik,bkp->ibp/dot_general | solution.py:51
  961.9 19.4 %fusion.93 = f32[8,3,64,128]{3,1,2,0:T(4,128)S(1)} fusion(f32[8,3,64,128]{3,1,2,0:T(4,128)S(1)} %get-tuple-element.556, s32[]{:T(128)} %get-tuple-element.555, f32[64,128,128]{2,1,0:T(8,128)S(1)} %fusion.92, f32[128]{0:T(128)S(1)} %get-tuple-element.568, f32[64,128]{1,0:T(8,128)S(1)} %dynamic-slice_bitcast_fusion.2, f32[3,128]{1,0:T(4,128)S(1)} %get-tuple-element.569), kind=kOutput, calls=%fused_computation.27.clone.1 | convolution fusion | flops 39845888 | bytes 4360708 | tf_op jit(solution)/shard_map/while/body/eval_jaxpr/ik,bkp->ibp/dot_general | solution.py:51
  988.9 19.4 %fusion.93 = f32[8,3,64,128]{3,1,2,0:T(4,128)S(1)} fusion(f32[8,3,64,128]{3,1,2,0:T(4,128)S(1)} %get-tuple-element.556, s32[]{:T(128)} %get-tuple-element.555, f32[64,128,128]{2,1,0:T(8,128)S(1)} %fusion.92, f32[128]{0:T(128)S(1)} %get-tuple-element.568, f32[64,128]{1,0:T(8,128)S(1)} %dynamic-slice_bitcast_fusion.2, f32[3,128]{1,0:T(4,128)S(1)} %get-tuple-element.569), kind=kOutput, calls=%fused_computation.27.clone.1 | convolution fusion | flops 39845888 | bytes 4360708 | tf_op jit(solution)/shard_map/while/body/eval_jaxpr/ik,bkp->ibp/dot_general | solution.py:51
  1016.0 19.4 %fusion.93 = f32[8,3,64,128]{3,1,2,0:T(4,128)S(1)} fusion(f32[8,3,64,128]{3,1,2,0:T(4,128)S(1)} %get-tuple-element.556, s32[]{:T(128)} %get-tuple-element.555, f32[64,128,128]{2,1,0:T(8,128)S(1)} %fusion.92, f32[128]{0:T(128)S(1)} %get-tuple-element.568, f32[64,128]{1,0:T(8,128)S(1)} %dynamic-slice_bitcast_fusion.2, f32[3,128]{1,0:T(4,128)S(1)} %get-tuple-element.569), kind=kOutput, calls=%fused_computation.27.clone.1 | convolution fusion | flops 39845888 | bytes 4360708 | tf_op jit(solution)/shard_map/while/body/eval_jaxpr/ik,bkp->ibp/dot_general | solution.py:51
  (539 shorter events, 503.3 us)
Async XLA Ops:
  0.0 814.3 %copy-start = (f32[16,128,128]{2,1,0:T(8,128)S(1)}, f32[16,128,128]{2,1,0:T(8,128)}, u32[]{:S(2)}) copy-start(f32[16,128,128]{2,1,0:T(8,128)} %param.33) | copy-start | bytes 3145732
  0.0 3.7 copy-start.1
  2.2 3.2 copy-start.8
  2.2 3.1 copy-start.10
  2.2 3.1 copy-start.12
  5.3 228.7 %copy-start.16 = (s32[16,8]{0,1:T(8,128)S(1)}, s32[16,8]{0,1:T(8,128)}, u32[]{:S(2)}) copy-start(s32[16,8]{0,1:T(8,128)} %param.35) | copy-start | bytes 1540
  229.0 20.7 %copy-start.9 = (s32[512,32]{0,1:T(8,128)S(1)}, s32[512,32]{0,1:T(8,128)}, u32[]{:S(2)}) copy-start(s32[512,32]{0,1:T(8,128)} %param.36) | copy-start | bytes 196612
  229.7 521.1 %collective-permute-start = (f32[256,128]{1,0:T(8,128)}, f32[256,128]{1,0:T(8,128)}, u32[]{:S(2)}, u32[]{:S(2)}) collective-permute-start(f32[256,128]{1,0:T(8,128)} %bitcast.66), channel_id=1, source_target_pairs={{0,1},{1,2},{2,3},{3,4},{4,5},{5,6},{6,7},{7,8},{8,9},{9,10},{10,1... | collective-permute-start | bytes 393224 | tf_op jit(solution)/shard_map/ppermute | solution.py:26
  232.7 518.1 %collective-permute-start.1 = (f32[256,128]{1,0:T(8,128)}, f32[256,128]{1,0:T(8,128)}, u32[]{:S(2)}, u32[]{:S(2)}) collective-permute-start(f32[256,128]{1,0:T(8,128)} %bitcast.68), channel_id=1, source_target_pairs={{1,0},{2,1},{3,2},{4,3},{5,4},{6,5},{7,6},{8,7},{9,8},{10,9},{11,1... | collective-permute-start | bytes 393224 | tf_op jit(solution)/shard_map/ppermute | solution.py:28
  235.4 515.4 %all-to-all-start = ((f32[16,8,128]{2,1,0:T(8,128)}), f32[16,8,128]{2,1,0:T(8,128)S(1)}, u32[]{:S(2)}, u32[]{:S(2)}) async-start(f32[16,8,128]{2,1,0:T(8,128)} %bitcast.69), calls=%async_computation | async-start | bytes 131072 | tf_op jit(solution)/shard_map/all_to_all | solution.py:156
  244.1 34.3 %copy-start.14 = (s32[8,128]{1,0:T(8,128)S(1)}, s32[8,128]{1,0:T(8,128)}, u32[]{:S(2)}) copy-start(s32[8,128]{1,0:T(8,128)} %param.39) | copy-start | bytes 12292
  244.7 41.0 %collective-permute-start.2 = (f32[6,4,128]{2,1,0:T(4,128)}, f32[6,4,128]{2,1,0:T(4,128)}, u32[]{:S(2)}, u32[]{:S(2)}) collective-permute-start(f32[6,4,128]{2,1,0:T(4,128)} %get-tuple-element.291), channel_id=1, source_target_pairs={{0,1},{1,2},{2,3},{3,4},{4,5},{5,6},{6,7},{7,8},{8,9},{9,10},{10,1... | collective-permute-start | bytes 36872 | tf_op jit(solution)/shard_map/ppermute | solution.py:26
  247.6 38.1 %collective-permute-start.3 = (f32[6,4,128]{2,1,0:T(4,128)}, f32[6,4,128]{2,1,0:T(4,128)}, u32[]{:S(2)}, u32[]{:S(2)}) collective-permute-start(f32[6,4,128]{2,1,0:T(4,128)} %get-tuple-element.292), channel_id=1, source_target_pairs={{1,0},{2,1},{3,2},{4,3},{5,4},{6,5},{7,6},{8,7},{9,8},{10,9},{11,1... | collective-permute-start | bytes 36872 | tf_op jit(solution)/shard_map/ppermute | solution.py:28
  250.0 28.6 %copy-start.6 = (f32[16,128,128]{2,1,0:T(8,128)S(1)}, f32[16,128,128]{2,1,0:T(8,128)}, u32[]{:S(2)}) copy-start(f32[16,128,128]{2,1,0:T(8,128)} %param.34) | copy-start | bytes 3145732
  250.0 29.5 %copy-start.4 = (f32[8,128,128]{2,1,0:T(8,128)S(1)}, f32[8,128,128]{2,1,0:T(8,128)}, u32[]{:S(2)}) copy-start(f32[8,128,128]{2,1,0:T(8,128)} %param.32) | copy-start | bytes 1572868
  251.8 28.9 %copy-start.13 = (s32[512,1]{0,1:T(1,128)S(1)}, s32[512,1]{0,1:T(1,128)}, u32[]{:S(2)}) copy-start(s32[512,1]{0,1:T(1,128)} %iota_add_fusion) | copy-start | bytes 6148
  251.8 28.9 %copy-start.15 = (s32[512,2]{0,1:T(2,128)S(1)}, s32[512,2]{0,1:T(2,128)}, u32[]{:S(2)}) copy-start(s32[512,2]{0,1:T(2,128)} %param.38) | copy-start | bytes 12292
  286.7 1.5 copy-start.17
  750.8 0.6 copy-start.7
  752.5 54.5 %copy-start.2 = (pred[512,32,16]{1,2,0:T(8,128)(4,1)S(1)}, pred[512,32,16]{1,2,0:T(8,128)(4,1)}, u32[]{:S(2)}) copy-start(pred[512,32,16]{1,2,0:T(8,128)(4,1)} %copy.53) | copy-start | bytes 786436
  814.3 4.4 copy-start.5
  814.3 4.4 copy-start.11
  1035.5 1.1 copy-start.3
where the time goes:
time: 1060 us; the launch traced here: 1040 us
  matrix products  457 us (43%)
  other arithmetic  285 us (27%)
  local copies, waits for them, and re-layouts  201 us (19%)
  loops' own time  53.5 us (5%)
  blocking collectives  23.3 us (2%)
  starting transfers between devices  17.3 us (2%)
    dot_general x8, matrix products, moments_of(): weights = jnp.einsum('ik,ibp->bkp', charge_dirs, charged, precision=highest)  163 us
    dot_general x8, matrix products, velocity_of(): return jnp.einsum('ik,bkp->ibp', velocity_dirs, scaled, precision=highest)  155 us
    reduce_sum x48, other arithmetic, cross_sum(): jnp.sum(first * kernel, axis=-1)  140 us
    reduce_sum x16, other arithmetic, cross_sum(): dist = jnp.sum(diff * diff, axis=0) + smoothing_sq  122 us
    dot_general x16, matrix products, features(): jnp.einsum('ik,ibp->bkp', frequencies, coords, precision=highest)  121 us
    gather x48, local copies, waits for them, and re-layouts, block(): src_charged = jnp.take(ext_charged, rows_here, axis=1)  88.2 us
    gather x1, local copies, waits for them, and re-layouts, shards(): leaf_locals = leaf_down + translate(far_maps, far_class, lookup[far_source])  54.4 us
    another operation x1, loops' own time, near_field(): pieces = lax.map(block, starts)  52.7 us
  transfers between devices with their start and end apart: 5, of which 0 were waited for; matrix products, arithmetic and copies ran while one was open for 41% of the time, Pallas kernels for 0%

commit v1 on v0

v1 whole, which is shorter than its diff:
```python
import functools
import math

import jax
import jax.numpy as jnp
import numpy as np
from jax import lax
from jax.experimental import pallas as pl
from jax.experimental.pallas import tpu as pltpu
from jax.sharding import PartitionSpec as P

HW = 4
highest = lax.Precision.HIGHEST
smoothing_sq = 0.25
inverse_four_pi = 0.25 / math.pi
GROUP = 16
ROWS = 8
f32 = jnp.float32
bf16 = jnp.bfloat16


def cosine_coefficients(degree):
    nodes = np.cos(np.pi * (np.arange(4000) + 0.5) / 4000)
    square = (nodes + 1) / 8
    fit = np.polynomial.chebyshev.Chebyshev.fit(
        square, np.cos(2 * np.pi * np.sqrt(square)), degree, domain=[0, 0.25]
    )
    return [float(c) for c in fit.convert(kind=np.polynomial.Polynomial).coef]


cos_coef = cosine_coefficients(5)


def cos_turns(turns):
    rest = turns - jnp.round(turns)
    square = rest * rest
    value = jnp.full_like(square, cos_coef[-1])
    for c in cos_coef[-2::-1]:
        value = value * square + c
    return value


def split3(x):
    h = x.astype(bf16).astype(f32)
    rest = x - h
    m = rest.astype(bf16).astype(f32)
    return h, m, rest - m


def split3_outside(x):
    h = lax.reduce_precision(x, 8, 7)
    m = lax.reduce_precision(x - h, 8, 7)
    return h, m, lax.reduce_precision(x - h - m, 8, 7)


def nt(a, b):
    return lax.dot_general(a, b, (((1,), (1,)), ((), ())), preferred_element_type=f32)


def tn(a, b):
    return lax.dot_general(a, b, (((0,), (0,)), ((), ())), preferred_element_type=f32)


def pieces(out):
    return out[0:8] + out[8:16] + out[16:24]


def moments_kernel(pq_ref, freq_ref, dirs_ref, moment_ref, basis_ref):
    def pair(j, _):
        stacks, lhs = [], []
        for o in range(2):
            h, m, l = split3(pq_ref[2 * j + o])
            stacks.append(jnp.concatenate([h, m, l, h, m, h], axis=0).astype(bf16))
            lhs.append(jnp.concatenate([h, m, l, jnp.zeros_like(h)], axis=0).astype(bf16))
        turns = jnp.dot(
            freq_ref[...], jnp.concatenate(stacks, axis=1), preferred_element_type=f32
        )
        basis = cos_turns(turns)
        high = basis.astype(bf16)
        low = (basis - high.astype(f32)).astype(bf16)
        for o in range(2):
            both = jnp.concatenate(
                [high[:, o * 128 : (o + 1) * 128], low[:, o * 128 : (o + 1) * 128]], axis=0
            )
            basis_ref[2 * j + o] = both
            got = pieces(nt(lhs[o], both))
            got = got[:, :128] + got[:, 128:]
            moment_ref[pl.ds(2 * j + o, 1), :] = jnp.sum(
                got * dirs_ref[...], axis=0, keepdims=True
            )
        return 0

    lax.fori_loop(0, GROUP // 2, pair, 0, unroll=4)


def leaf_moments_of(pq, freq, dirs):
    boxes = pq.shape[0]
    return pl.pallas_call(
        moments_kernel,
        grid=(boxes // GROUP,),
        in_specs=[
            pl.BlockSpec((GROUP, ROWS, 128), lambda i: (i, 0, 0)),
            pl.BlockSpec(freq.shape, lambda i: (0, 0)),
            pl.BlockSpec(dirs.shape, lambda i: (0, 0)),
        ],
        out_specs=[
            pl.BlockSpec((GROUP, 128), lambda i: (i, 0)),
            pl.BlockSpec((GROUP, 256, 128), lambda i: (i, 0, 0)),
        ],
        out_shape=[
            jax.ShapeDtypeStruct((boxes, 128), f32),
            jax.ShapeDtypeStruct((boxes, 256, 128), bf16),
        ],
        compiler_params=pltpu.CompilerParams(vmem_limit_bytes=32 << 20),
        cost_estimate=pl.CostEstimate(
            flops=boxes * 128 * 128 * 96, bytes_accessed=boxes * 72000, transcendentals=0
        ),
        name="leaf_moments",
    )(pq, freq, dirs)


def near_kernel(near_ref, ext_ref, out_ref, source_ref, target_ref, charge_ref):
    row = lax.broadcasted_iota(jnp.int32, (8, 128), 0)

    def prepare(s, _):
        v = ext_ref[s]
        x, y, z = v[0:1], v[1:2], v[2:3]
        a0, a1, a2 = v[3:4], v[4:5], v[5:6]
        norm = x * x + y * y + z * z
        src = jnp.where(row < 3, v, jnp.where(row == 3, norm, jnp.where(row == 4, 1.0, 0.0)))
        tgt = jnp.where(
            row < 3,
            -2.0 * v,
            jnp.where(row == 3, 1.0, jnp.where(row == 4, norm + smoothing_sq, 0.0)),
        )
        zero = jnp.zeros_like(x)
        chg = jnp.concatenate(
            [a0, a1, a2, a1 * z - a2 * y, a2 * x - a0 * z, a0 * y - a1 * x, zero, zero], axis=0
        )
        h, m, l = split3(src)
        source_ref[s] = jnp.concatenate([h, m, l, h, m, h], axis=0).astype(bf16)
        h, m, l = split3(tgt)
        target_ref[s] = jnp.concatenate([h, h, h, m, m, l], axis=0).astype(bf16)
        h, m, l = split3(chg)
        charge_ref[s] = jnp.concatenate([h, m, l, jnp.zeros_like(h)], axis=0).astype(bf16)
        return 0

    lax.fori_loop(0, ext_ref.shape[0], prepare, 0, unroll=4)

    def box(b, _):
        rows = [b + HW, near_ref[2 * b], near_ref[2 * b + 1]]
        src = jnp.concatenate([source_ref[r] for r in rows], axis=1)
        dist = tn(target_ref[b + HW], src)
        inv = lax.rsqrt(dist)
        kern = inv * inv * inv
        high = kern.astype(bf16)
        low = (kern - high.astype(f32)).astype(bf16)
        chg = [charge_ref[r] for r in rows]
        out_ref[b] = pieces(
            nt(jnp.concatenate(chg + chg, axis=1), jnp.concatenate([high, low], axis=1))
        )
        return 0

    lax.fori_loop(0, out_ref.shape[0], box, 0, unroll=4)


def near_sums(near_rows, ext):
    boxes = near_rows.shape[0] // 2
    total = ext.shape[0]
    return pl.pallas_call(
        near_kernel,
        grid_spec=pltpu.PrefetchScalarGridSpec(
            num_scalar_prefetch=1,
            grid=(1,),
            in_specs=[pl.BlockSpec(ext.shape, lambda i, n: (0, 0, 0))],
            out_specs=pl.BlockSpec((boxes, 8, 128), lambda i, n: (0, 0, 0)),
            scratch_shapes=[
                pltpu.VMEM((total, 48, 128), bf16),
                pltpu.VMEM((total, 48, 128), bf16),
                pltpu.VMEM((total, 32, 128), bf16),
            ],
        ),
        out_shape=jax.ShapeDtypeStruct((boxes, 8, 128), f32),
        compiler_params=pltpu.CompilerParams(vmem_limit_bytes=48 << 20),
        cost_estimate=pl.CostEstimate(
            flops=boxes * 3 * 128 * 128 * 160, bytes_accessed=boxes * 8192, transcendentals=0
        ),
        name="near_sums",
    )(near_rows, ext)


def far_kernel(
    index_ref, table_ref, maps_ref, down_ref, dirs_ref, basis_ref, near_ref, pq_ref, out_ref, moved_ref
):
    size = table_ref.shape[0]
    step = pl.program_id(0)

    @pl.when(step == 0)
    def _():
        def one(n, _):
            moved_ref[pl.ds(n * size, size), :] = lax.dot_general(
                table_ref[...],
                maps_ref[n],
                (((1,), (1,)), ((), ())),
                preferred_element_type=f32,
                precision=highest,
            )
            return 0

        lax.fori_loop(0, maps_ref.shape[0], one, 0)

    links = index_ref.shape[0] // (pl.num_programs(0) * GROUP)

    def box(j, _):
        start = (step * GROUP + j) * links
        sums = [down_ref[pl.ds(j, 1), :], None, None, None]
        for l in range(links):
            got = moved_ref[pl.ds(index_ref[start + l], 1), :]
            sums[l % 4] = got if sums[l % 4] is None else sums[l % 4] + got
        local = (sums[0] + sums[1]) + (sums[2] + sums[3])
        h, m, l = split3(dirs_ref[...] * local)
        lhs = jnp.concatenate([h, m, l, jnp.zeros_like(h)], axis=0).astype(bf16)
        far = pieces(
            jnp.dot(
                jnp.concatenate([lhs, lhs], axis=1), basis_ref[j], preferred_element_type=f32
            )
        )
        pq = pq_ref[j]
        near = near_ref[j]
        x, y, z, keep = pq[0:1], pq[1:2], pq[2:3], pq[6:7]
        s0, s1, s2 = near[0:1], near[1:2], near[2:3]
        first = s1 * z - s2 * y - near[3:4]
        second = s2 * x - s0 * z - near[4:5]
        third = s0 * y - s1 * x - near[5:6]
        for i, value in enumerate((first, second, third)):
            out_ref[i, pl.ds(j, 1), :] = (far[i : i + 1] + value * inverse_four_pi) * keep
        return 0

    lax.fori_loop(0, GROUP, box, 0, unroll=4)


def far_velocity_of(index, table, maps, down, dirs, basis, near, pq):
    boxes = pq.shape[0]
    return pl.pallas_call(
        far_kernel,
        grid_spec=pltpu.PrefetchScalarGridSpec(
            num_scalar_prefetch=1,
            grid=(boxes // GROUP,),
            in_specs=[
                pl.BlockSpec(table.shape, lambda i, n: (0, 0)),
                pl.BlockSpec(maps.shape, lambda i, n: (0, 0, 0)),
                pl.BlockSpec((GROUP, 128), lambda i, n: (i, 0)),
                pl.BlockSpec(dirs.shape, lambda i, n: (0, 0)),
                pl.BlockSpec((GROUP, 256, 128), lambda i, n: (i, 0, 0)),
                pl.BlockSpec((GROUP, 8, 128), lambda i, n: (i, 0, 0)),
                pl.BlockSpec((GROUP, 8, 128), lambda i, n: (i, 0, 0)),
            ],
            out_specs=pl.BlockSpec((3, GROUP, 128), lambda i, n: (0, i, 0)),
            scratch_shapes=[pltpu.VMEM((maps.shape[0] * table.shape[0], 128), f32)],
        ),
        out_shape=jax.ShapeDtypeStruct((3, boxes, 128), f32),
        compiler_params=pltpu.CompilerParams(vmem_limit_bytes=48 << 20),
        name="far_velocity",
    )(index, table, maps, down, dirs, basis, near, pq)


def padded(cells, axis, width):
    count = lax.axis_size(axis)
    ends = count - 1
    head = cells[:width]
    tail = cells[cells.shape[0] - width :]
    return jnp.concatenate(
        [
            lax.ppermute(tail, axis, [(i, i + 1) for i in range(ends)]),
            cells,
            lax.ppermute(head, axis, [(i + 1, i) for i in range(ends)]),
        ],
        axis=0,
    )


def upward(maps, child):
    grouped_child = child.reshape(-1, 8, child.shape[-1])
    return jnp.einsum("jkl,qjl->qk", maps, grouped_child, precision=highest)


def downward(maps, parent):
    return jnp.einsum("jkl,ql->qjk", maps, parent, precision=highest).reshape(-1, parent.shape[-1])


def coarse_translate(maps, classes, sources):
    onehot = (
        classes[:, :, None] == jnp.arange(maps.shape[0], dtype=jnp.int32)[None, None, :]
    ).astype(f32)
    summed = jnp.einsum("ten,ek->ntk", onehot, sources, precision=highest)
    return jnp.einsum("nkl,ntl->tk", maps, summed, precision=highest)


def shards(
    positions,
    strengths,
    counts,
    frequencies,
    phases,
    charge_dirs,
    velocity_dirs,
    up_maps,
    down_maps,
    far_maps,
    coarse_maps,
    send_boxes,
    far_source,
    far_class,
    near_source,
    coarse_class,
):
    axis = ("curve", "sub")
    boxes, slots = positions.shape[1:]
    coeffs = frequencies.shape[1]
    slot_index = jnp.arange(slots, dtype=jnp.int32)
    occupied = (slot_index[None, :] < counts[:, None]).astype(f32)
    charged = strengths * occupied[None]
    pq = jnp.stack(
        [positions[0], positions[1], positions[2], charged[0], charged[1], charged[2], occupied,
         jnp.ones_like(occupied)],
        axis=1,
    )
    ext = padded(pq, axis, HW)
    none = jnp.zeros((coeffs,), f32)
    turn = 1.0 / (2.0 * math.pi)
    waves = jnp.stack(
        [frequencies[0] * turn, frequencies[1] * turn, frequencies[2] * turn, none, none, none, none,
         phases * turn],
        axis=1,
    )
    h, m, l = split3_outside(waves)
    freq = jnp.concatenate([h, h, h, m, m, l], axis=1).astype(bf16)
    dirs = jnp.stack([none, none, none, charge_dirs[0], charge_dirs[1], charge_dirs[2], none, none])
    leaf_moments, basis = leaf_moments_of(pq, freq, dirs)
    nearby_moments = padded(leaf_moments, axis, boxes // 2)
    parcel = leaf_moments[send_boxes]
    received = lax.all_to_all(parcel, axis, split_axis=0, concat_axis=0, tiled=True)
    top_moments = upward(up_maps, upward(up_maps, leaf_moments))
    coarse_moments = lax.all_gather(top_moments, axis, axis=0, tiled=True)
    near = near_sums(near_source.reshape(-1), ext)
    coarse_locals = coarse_translate(coarse_maps, coarse_class, coarse_moments)
    leaf_down = downward(down_maps, downward(down_maps, coarse_locals))
    table = jnp.concatenate([nearby_moments, received.reshape(-1, coeffs)], axis=0)
    index = (far_class * table.shape[0] + far_source).reshape(-1)
    vel_dirs = jnp.concatenate([velocity_dirs, jnp.zeros((5, coeffs), f32)], axis=0)
    return far_velocity_of(index, table, far_maps, leaf_down, vel_dirs, basis, near, pq)


def solution(mesh):
    boxed = P(None, ("runs", "curve", "sub"), None)
    listed = P(("runs", "curve", "sub"), None)
    return jax.shard_map(
        shards,
        mesh=mesh,
        in_specs=(boxed, boxed, P(("runs", "curve", "sub")), *([P()] * 8), *([listed] * 5)),
        out_specs=boxed,
        check_vma=False,
    )
```

time: 1060 us -> 304 us (0.29); the launches traced: 1040 us -> 302 us
  matrix products: 457 us -> 6.27 us
  other arithmetic: 285 us -> 6.25 us
  Pallas kernels: 0 us -> 227 us
  local copies, waits for them, and re-layouts: 201 us -> 21.8 us
  loops' own time: 53.5 us -> 0 us
    dot_general x34 -> x0, matrix products: 451 us -> none  [the longest x8 163 us: moments_of(): weights = jnp.einsum('ik,ibp->bkp', charge_dirs, charged, precision=highest)]
    reduce_sum x64 -> x0, other arithmetic: 262 us -> none  [the longest x48 140 us: cross_sum(): jnp.sum(first * kernel, axis=-1)]
    pallas_call x0 -> x3, Pallas kernels: none -> 227 us  [the longest x1 115 us: near_sums(): pl.pallas_call(near_kernel, grid_spec=pltpu.PrefetchScalarGridSpec(num_sc...]
    gather x97 -> x0, local copies, waits for them, and re-layouts: 172 us -> none  [the longest x48 88.2 us: block(): src_charged = jnp.take(ext_charged, rows_here, axis=1)]
    another operation x3 -> x0, loops' own time: 53.5 us -> none  [the longest x1 52.7 us: near_field(): pieces = lax.map(block, starts)]
    dynamic_slice x64 -> x0, local copies, waits for them, and re-layouts: 12 us -> none  [the longest x16 10.3 us: near_field(): pieces = lax.map(block, starts)]
  transfers between devices with their start and end apart: 5 -> 5, of which waited for: 0 -> 0; matrix products, arithmetic and copies ran while one was open for 41% -> 5% of each run, Pallas kernels for 0% -> 59%
where the time goes in v1:
time: 304 us; the launch traced here: 302 us
  Pallas kernels  227 us (75%)
  blocking collectives  23.2 us (8%)
  local copies, waits for them, and re-layouts  21.8 us (7%)
  starting transfers between devices  17.3 us (6%)
  matrix products  6.27 us (2%)
  other arithmetic  6.25 us (2%)
    pallas_call x1, Pallas kernels, near_sums(): pl.pallas_call(near_kernel, grid_spec=pltpu.PrefetchScalarGridSpec(num_sc...  115 us
    pallas_call x1, Pallas kernels, leaf_moments_of(): pl.pallas_call(moments_kernel, grid=(boxes // GROUP,), in_specs=[pl.Block...  62.7 us
    pallas_call x1, Pallas kernels, far_velocity_of(): pl.pallas_call(far_kernel, grid_spec=pltpu.PrefetchScalarGridSpec(num_sca...  49.2 us
    all_gather x1, blocking collectives, shards(): coarse_moments = lax.all_gather(top_moments, axis, axis=0, tiled=True)  23.2 us
    all_to_all x1, starting transfers between devices, shards(): lax.all_to_all(parcel, axis, split_axis=0, concat_axis=0, tiled=True)  8.7 us
    another operation x2, local copies, waits for them, and re-layouts, shards(): jnp.stack([positions[0], positions[1], positions[2], charged[0], charged[...  6.27 us
  transfers between devices with their start and end apart: 5, of which 0 were waited for; matrix products, arithmetic and copies ran while one was open for 5% of the time, Pallas kernels for 59%

profile of v1, /device:TPU:0, one launch (start us, length us, event | category | flops | bytes accessed | tf_op | source)
XLA Modules:
  0.0 302.2 jit_solution(17942555148589962303)
XLA Ops:
  0.0 2.2 compare_convert_fusion
  2.2 0.8 fusion.2
  3.0 1.2 broadcast_multiply_fusion
  4.2 0.9 fusion.12
  5.1 0.9 fusion.13
  6.0 0.8 stack_broadcast_in_dim.6
  6.9 5.4 %stack.19.pq_ref = f32[512,8,128]{2,1,0:T(8,128)S(1)} concatenate(f32[512,1,128]{2,1,0:T(1,128)} %bitcast.58, f32[512,1,128]{2,1,0:T(1,128)} %bitcast.59, f32[512,1,128]{2,1,0:T(1,128)} %bitcast.57, f32[512,1,128]{2,1,0:T(1,128)} %bitcast.56, f32[512,1,128]{2,1,0:T(1,128)} %bitcast.55, f32[512,1,128]{2,1,0:T(1,128)} %bitcast.54, f32[512,1,128]{2,1,0:T(1,128)S(1)} %compare_convert_fusion, ...), dimensions={1} | concatenate | bytes 4194304 | tf_op jit(solution)/shard_map/stack | solution.py:323
  12.9 3.0 collective-permute-start.2
  15.9 1.3 collective-permute-start.3
  17.7 62.7 %leaf_moments.1 = (f32[512,128]{1,0:T(8,128)S(1)}, bf16[512,256,128]{2,1,0:T(8,128)(2,1)}) custom-call(f32[512,8,128]{2,1,0:T(8,128)S(1)} %stack.19.pq_ref, bf16[128,48]{1,0:T(8,128)(2,1)S(1)} %copy.39.freq_ref, f32[8,128]{1,0:T(8,128)S(1)} %pad_maximum_fusion.2.dirs_ref), custom_call_target="tpu_custom_call" | custom-call | flops 805306368 | bytes 36864000 | tf_op jit(solution)/shard_map/leaf_moments/pallas_call | solution.py:98
  80.5 1.2 gather_fusion
  81.7 8.7 %all-to-all-start = ((f32[16,8,128]{2,1,0:T(8,128)}), f32[16,8,128]{2,1,0:T(8,128)S(1)}, u32[]{:S(2)}, u32[]{:S(2)}) async-start(f32[16,8,128]{2,1,0:T(8,128)} %bitcast.12), calls=%async_computation | async-start | bytes 131072 | tf_op jit(solution)/shard_map/all_to_all | solution.py:342
  91.2 3.1 %collective-permute-start = (f32[256,128]{1,0:T(8,128)}, f32[256,128]{1,0:T(8,128)}, u32[]{:S(2)}, u32[]{:S(2)}) collective-permute-start(f32[256,128]{1,0:T(8,128)} %get-tuple-element.17), channel_id=1, source_target_pairs={{0,1},{1,2},{2,3},{3,4},{4,5},{5,6},{6,7},{7,8},{8,9},{9,10},{10,1... | collective-permute-start | bytes 393224 | tf_op jit(solution)/shard_map/ppermute | solution.py:274
  94.2 1.3 collective-permute-start.1
  95.6 1.7 convolution_bitcast_fusion
  97.3 1.6 convolution_bitcast_fusion.1
  98.8 23.2 %all_gather.3 = f32[128,128]{1,0:T(8,128)S(1)} all-gather(f32[8,128]{1,0:T(8,128)S(1)} %convolution_bitcast_fusion.1), channel_id=1, replica_groups=mesh['runs'=2,'curve'=4,'sub'=4] {'curve','sub'}, dimensions={0}, use_global_device_ids=true | all-gather | bytes 69632 | tf_op jit(solution)/shard_map/all_gather | solution.py:344
  122.3 0.9 fusion.3
  123.7 1.4 fusion.5
  125.1 0.8 copy.36
  126.0 1.1 reshape.103.index_ref
  127.1 0.9 copy.46
  127.9 1.1 reshape.107.near_ref
  129.0 1.8 copy.59
  130.8 0.9 pad_maximum_fusion.ext_ref
  131.7 115.1 %near_sums.1.near_ref = f32[512,8,128]{2,1,0:T(8,128)S(1)} custom-call(s32[1024]{0:T(1024)S(1)} %reshape.107.near_ref, f32[520,8,128]{2,1,0:T(8,128)S(1)} %pad_maximum_fusion.ext_ref), custom_call_target="tpu_custom_call" | custom-call | flops 4026531840 | bytes 4194304 | tf_op jit(solution)/shard_map/near_sums/pallas_call | solution.py:170
  246.8 1.3 copy-done.1
  248.2 1.0 pad_maximum_fusion.1.table_ref
  249.2 1.6 copy-done.2
  250.8 0.9 copy-done.3
  251.7 1.2 copy-done.4
  253.0 49.2 %far_velocity.1 = f32[3,512,128]{2,1,0:T(8,128)} custom-call(s32[16384]{0:T(1024)S(1)} %reshape.103.index_ref, f32[1152,128]{1,0:T(8,128)S(1)} %pad_maximum_fusion.1.table_ref, f32[16,128,128]{2,1,0:T(8,128)S(1)} %copy-done.4, f32[512,128]{1,0:T(8,128)S(1)} %bitcast.53, f32[8,128]{1,0:T(8,128)S(1)} %concatenate.15.dirs_ref, ...), custom_call_target="tpu_custom_call" | custom-call | tf_op jit(solution)/shard_map/far_velocity/pallas_call | solution.py:244
  (58 shorter events, 2.6 us)
Async XLA Ops:
  0.0 122.2 %copy-start = (f32[16,128,128]{2,1,0:T(8,128)S(1)}, f32[16,128,128]{2,1,0:T(8,128)}, u32[]{:S(2)}) copy-start(f32[16,128,128]{2,1,0:T(8,128)} %param.26) | copy-start | bytes 3145732
  0.0 5.1 %copy-start.6 = (f32[3,512,128]{2,1,0:T(8,128)S(1)}, f32[3,512,128]{2,1,0:T(8,128)}, u32[]{:S(2)}) copy-start(f32[3,512,128]{2,1,0:T(8,128)} %param.16) | copy-start | bytes 2359300
  6.9 10.3 %copy-start.15 = (f32[128]{0:T(128)S(1)}, f32[128]{0:T(128)}, u32[]{:S(2)}) copy-start(f32[128]{0:T(128)} %param.20) | copy-start | bytes 1540
  6.9 10.3 %copy-start.14 = (f32[3,128]{1,0:T(4,128)S(1)}, f32[3,128]{1,0:T(4,128)}, u32[]{:S(2)}) copy-start(f32[3,128]{1,0:T(4,128)} %param.19) | copy-start | bytes 4612
  6.9 10.3 %copy-start.11 = (s32[16,8]{0,1:T(8,128)S(1)}, s32[16,8]{0,1:T(8,128)}, u32[]{:S(2)}) copy-start(s32[16,8]{0,1:T(8,128)} %param.27) | copy-start | bytes 1540
  6.9 10.8 %copy-start.13 = (f32[3,128]{1,0:T(4,128)S(1)}, f32[3,128]{1,0:T(4,128)}, u32[]{:S(2)}) copy-start(f32[3,128]{1,0:T(4,128)} %param.21) | copy-start | bytes 4612
  12.9 117.9 %collective-permute-start.2 = (f32[4,8,128]{2,1,0:T(8,128)}, f32[4,8,128]{2,1,0:T(8,128)}, u32[]{:S(2)}, u32[]{:S(2)}) collective-permute-start(f32[4,8,128]{2,1,0:T(8,128)} %get-tuple-element.9), channel_id=1, source_target_pairs={{0,1},{1,2},{2,3},{3,4},{4,5},{5,6},{6,7},{7,8},{8,9},{9,10},{10,1... | collective-permute-start | bytes 49160 | tf_op jit(solution)/shard_map/ppermute | solution.py:274
  15.9 115.0 %collective-permute-start.3 = (f32[4,8,128]{2,1,0:T(8,128)}, f32[4,8,128]{2,1,0:T(8,128)}, u32[]{:S(2)}, u32[]{:S(2)}) collective-permute-start(f32[4,8,128]{2,1,0:T(8,128)} %get-tuple-element.10), channel_id=1, source_target_pairs={{1,0},{2,1},{3,2},{4,3},{5,4},{6,5},{7,6},{8,7},{9,8},{10,9},{11,1... | collective-permute-start | bytes 49160 | tf_op jit(solution)/shard_map/ppermute | solution.py:276
  17.6 77.9 %copy-start.10 = (s32[8,128]{1,0:T(8,128)S(1)}, s32[8,128]{1,0:T(8,128)}, u32[]{:S(2)}) copy-start(s32[8,128]{1,0:T(8,128)} %param.31) | copy-start | bytes 12292
  81.7 166.5 %all-to-all-start = ((f32[16,8,128]{2,1,0:T(8,128)}), f32[16,8,128]{2,1,0:T(8,128)S(1)}, u32[]{:S(2)}, u32[]{:S(2)}) async-start(f32[16,8,128]{2,1,0:T(8,128)} %bitcast.12), calls=%async_computation | async-start | bytes 131072 | tf_op jit(solution)/shard_map/all_to_all | solution.py:342
  90.4 32.8 %copy-start.5 = (f32[8,128,128]{2,1,0:T(8,128)S(1)}, f32[8,128,128]{2,1,0:T(8,128)}, u32[]{:S(2)}) copy-start(f32[8,128,128]{2,1,0:T(8,128)} %param.24) | copy-start | bytes 1572868
  91.1 33.9 %copy-start.7 = (s32[512,32]{0,1:T(8,128)S(1)}, s32[512,32]{0,1:T(8,128)}, u32[]{:S(2)}) copy-start(s32[512,32]{0,1:T(8,128)} %param.28) | copy-start | bytes 196612
  91.2 33.9 %copy-start.8 = (s32[512,32]{0,1:T(8,128)S(1)}, s32[512,32]{0,1:T(8,128)}, u32[]{:S(2)}) copy-start(s32[512,32]{0,1:T(8,128)} %param.29) | copy-start | bytes 196612
  91.2 157.0 %collective-permute-start = (f32[256,128]{1,0:T(8,128)}, f32[256,128]{1,0:T(8,128)}, u32[]{:S(2)}, u32[]{:S(2)}) collective-permute-start(f32[256,128]{1,0:T(8,128)} %get-tuple-element.17), channel_id=1, source_target_pairs={{0,1},{1,2},{2,3},{3,4},{4,5},{5,6},{6,7},{7,8},{8,9},{9,10},{10,1... | collective-permute-start | bytes 393224 | tf_op jit(solution)/shard_map/ppermute | solution.py:274
  94.2 153.9 %collective-permute-start.1 = (f32[256,128]{1,0:T(8,128)}, f32[256,128]{1,0:T(8,128)}, u32[]{:S(2)}, u32[]{:S(2)}) collective-permute-start(f32[256,128]{1,0:T(8,128)} %get-tuple-element.18), channel_id=1, source_target_pairs={{1,0},{2,1},{3,2},{4,3},{5,4},{6,5},{7,6},{8,7},{9,8},{10,9},{11,1... | collective-permute-start | bytes 393224 | tf_op jit(solution)/shard_map/ppermute | solution.py:276
  95.5 29.6 %copy-start.12 = (f32[3,128]{1,0:T(4,128)S(1)}, f32[3,128]{1,0:T(4,128)}, u32[]{:S(2)}) copy-start(f32[3,128]{1,0:T(4,128)} %param.22) | copy-start | bytes 4612
  97.3 29.8 %copy-start.9 = (s32[512,2]{0,1:T(2,128)S(1)}, s32[512,2]{0,1:T(2,128)}, u32[]{:S(2)}) copy-start(s32[512,2]{0,1:T(2,128)} %param.30) | copy-start | bytes 12292
  246.8 1.4 copy-start.1
  249.2 1.6 copy-start.2
  250.8 0.9 copy-start.3
  251.7 1.2 copy-start.4

commit v2 on v1

--- a/solution.py
+++ b/solution.py
@@ -13,7 +13,6 @@
 highest = lax.Precision.HIGHEST
 smoothing_sq = 0.25
 inverse_four_pi = 0.25 / math.pi
-GROUP = 16
 ROWS = 8
 f32 = jnp.float32
 bf16 = jnp.bfloat16
@@ -65,55 +64,41 @@
     return out[0:8] + out[8:16] + out[16:24]
 
 
-def moments_kernel(pq_ref, freq_ref, dirs_ref, moment_ref, basis_ref):
-    def pair(j, _):
-        stacks, lhs = [], []
-        for o in range(2):
-            h, m, l = split3(pq_ref[2 * j + o])
-            stacks.append(jnp.concatenate([h, m, l, h, m, h], axis=0).astype(bf16))
-            lhs.append(jnp.concatenate([h, m, l, jnp.zeros_like(h)], axis=0).astype(bf16))
-        turns = jnp.dot(
-            freq_ref[...], jnp.concatenate(stacks, axis=1), preferred_element_type=f32
-        )
-        basis = cos_turns(turns)
-        high = basis.astype(bf16)
-        low = (basis - high.astype(f32)).astype(bf16)
-        for o in range(2):
-            both = jnp.concatenate(
-                [high[:, o * 128 : (o + 1) * 128], low[:, o * 128 : (o + 1) * 128]], axis=0
-            )
-            basis_ref[2 * j + o] = both
-            got = pieces(nt(lhs[o], both))
-            got = got[:, :128] + got[:, 128:]
-            moment_ref[pl.ds(2 * j + o, 1), :] = jnp.sum(
-                got * dirs_ref[...], axis=0, keepdims=True
-            )
-        return 0
-
-    lax.fori_loop(0, GROUP // 2, pair, 0, unroll=4)
+def stacks_of(tile):
+    h, m, l = split3(tile)
+    angles = jnp.concatenate([h, m, l, h, m, h], axis=0).astype(bf16)
+    return angles, jnp.concatenate([h, m, l, jnp.zeros_like(h)], axis=0).astype(bf16)
+
+
+def split_product(lhs, rhs):
+    high = rhs.astype(bf16)
+    low = (rhs - high.astype(f32)).astype(bf16)
+    out = jnp.dot(
+        jnp.concatenate([lhs, lhs], axis=1),
+        jnp.concatenate([high, low], axis=0),
+        preferred_element_type=f32,
+    )
+    return pieces(out)
+
+
+def moments_kernel(pq_ref, freq_ref, dirs_ref, moment_ref):
+    def box(b, _):
+        angles, charges = stacks_of(pq_ref[b])
+        got = split_product(charges, cos_turns(tn(angles, freq_ref[...])))
+        moment_ref[pl.ds(b, 1), :] = jnp.sum(got * dirs_ref[...], axis=0, keepdims=True)
+        return 0
+
+    lax.fori_loop(0, pq_ref.shape[0], box, 0, unroll=32)
 
 
 def leaf_moments_of(pq, freq, dirs):
     boxes = pq.shape[0]
     return pl.pallas_call(
         moments_kernel,
-        grid=(boxes // GROUP,),
-        in_specs=[
-            pl.BlockSpec((GROUP, ROWS, 128), lambda i: (i, 0, 0)),
-            pl.BlockSpec(freq.shape, lambda i: (0, 0)),
-            pl.BlockSpec(dirs.shape, lambda i: (0, 0)),
-        ],
-        out_specs=[
-            pl.BlockSpec((GROUP, 128), lambda i: (i, 0)),
-            pl.BlockSpec((GROUP, 256, 128), lambda i: (i, 0, 0)),
-        ],
-        out_shape=[
-            jax.ShapeDtypeStruct((boxes, 128), f32),
-            jax.ShapeDtypeStruct((boxes, 256, 128), bf16),
-        ],
+        out_shape=jax.ShapeDtypeStruct((boxes, 128), f32),
         compiler_params=pltpu.CompilerParams(vmem_limit_bytes=32 << 20),
         cost_estimate=pl.CostEstimate(
-            flops=boxes * 128 * 128 * 96, bytes_accessed=boxes * 72000, transcendentals=0
+            flops=boxes * 128 * 128 * 96, bytes_accessed=boxes * 8192, transcendentals=0
         ),
         name="leaf_moments",
     )(pq, freq, dirs)
@@ -150,18 +135,12 @@
     def box(b, _):
         rows = [b + HW, near_ref[2 * b], near_ref[2 * b + 1]]
         src = jnp.concatenate([source_ref[r] for r in rows], axis=1)
-        dist = tn(target_ref[b + HW], src)
-        inv = lax.rsqrt(dist)
-        kern = inv * inv * inv
-        high = kern.astype(bf16)
-        low = (kern - high.astype(f32)).astype(bf16)
-        chg = [charge_ref[r] for r in rows]
-        out_ref[b] = pieces(
-            nt(jnp.concatenate(chg + chg, axis=1), jnp.concatenate([high, low], axis=1))
-        )
-        return 0
-
-    lax.fori_loop(0, out_ref.shape[0], box, 0, unroll=4)
+        inv = lax.rsqrt(tn(src, target_ref[b + HW]))
+        charges = jnp.concatenate([charge_ref[r] for r in rows], axis=1)
+        out_ref[b] = split_product(charges, inv * inv * inv)
+        return 0
+
+    lax.fori_loop(0, out_ref.shape[0], box, 0, unroll=32)
 
 
 def near_sums(near_rows, ext):
@@ -190,78 +169,64 @@
 
 
 def far_kernel(
-    index_ref, table_ref, maps_ref, down_ref, dirs_ref, basis_ref, near_ref, pq_ref, out_ref, moved_ref
+    index_ref, table_ref, maps_ref, down_ref, freq_ref, dirs_ref, near_ref, pq_ref, out_ref, moved_ref
 ):
     size = table_ref.shape[0]
-    step = pl.program_id(0)
-
-    @pl.when(step == 0)
-    def _():
-        def one(n, _):
-            moved_ref[pl.ds(n * size, size), :] = lax.dot_general(
-                table_ref[...],
-                maps_ref[n],
-                (((1,), (1,)), ((), ())),
-                preferred_element_type=f32,
-                precision=highest,
-            )
-            return 0
-
-        lax.fori_loop(0, maps_ref.shape[0], one, 0)
-
-    links = index_ref.shape[0] // (pl.num_programs(0) * GROUP)
-
-    def box(j, _):
-        start = (step * GROUP + j) * links
-        sums = [down_ref[pl.ds(j, 1), :], None, None, None]
+    high = table_ref[...].astype(bf16)
+    both = jnp.concatenate([high, (table_ref[...] - high.astype(f32)).astype(bf16)], axis=1)
+
+    def one(n, _):
+        got = jnp.dot(both, maps_ref[n], preferred_element_type=f32)
+        moved_ref[pl.ds(pl.multiple_of(n * size, size), size), :] = got[:, :128] + got[:, 128:]
+        return 0
+
+    lax.fori_loop(0, maps_ref.shape[0], one, 0)
+    boxes = pq_ref.shape[0]
+    links = index_ref.shape[0] // boxes
+
+    def box(b, _):
+        sums = [down_ref[pl.ds(b, 1), :], None, None, None]
         for l in range(links):
-            got = moved_ref[pl.ds(index_ref[start + l], 1), :]
+            got = moved_ref[pl.ds(index_ref[b * links + l], 1), :]
             sums[l % 4] = got if sums[l % 4] is None else sums[l % 4] + got
         local = (sums[0] + sums[1]) + (sums[2] + sums[3])
-        h, m, l = split3(dirs_ref[...] * local)
-        lhs = jnp.concatenate([h, m, l, jnp.zeros_like(h)], axis=0).astype(bf16)
-        far = pieces(
-            jnp.dot(
-                jnp.concatenate([lhs, lhs], axis=1), basis_ref[j], preferred_element_type=f32
-            )
-        )
-        pq = pq_ref[j]
-        near = near_ref[j]
+        pq = pq_ref[b]
+        angles, _ = stacks_of(pq)
+        _, weights = stacks_of(dirs_ref[...] * local)
+        turns = jnp.dot(freq_ref[...], angles, preferred_element_type=f32)
+        far = split_product(weights, cos_turns(turns))
+        near = near_ref[b]
         x, y, z, keep = pq[0:1], pq[1:2], pq[2:3], pq[6:7]
         s0, s1, s2 = near[0:1], near[1:2], near[2:3]
         first = s1 * z - s2 * y - near[3:4]
         second = s2 * x - s0 * z - near[4:5]
         third = s0 * y - s1 * x - near[5:6]
         for i, value in enumerate((first, second, third)):
-            out_ref[i, pl.ds(j, 1), :] = (far[i : i + 1] + value * inverse_four_pi) * keep
-        return 0
-
-    lax.fori_loop(0, GROUP, box, 0, unroll=4)
-
-
-def far_velocity_of(index, table, maps, down, dirs, basis, near, pq):
+            out_ref[i, pl.ds(b, 1), :] = (far[i : i + 1] + value * inverse_four_pi) * keep
+        return 0
+
+    lax.fori_loop(0, boxes, box, 0, unroll=16)
+
+
+def far_velocity_of(index, table, maps, down, freq, dirs, near, pq):
     boxes = pq.shape[0]
+    whole = [
+        pl.BlockSpec(a.shape, functools.partial(lambda rank, i, n: (0,) * rank, a.ndim))
+        for a in (table, maps, down, freq, dirs, near, pq)
+    ]
     return pl.pallas_call(
         far_kernel,
         grid_spec=pltpu.PrefetchScalarGridSpec(
             num_scalar_prefetch=1,
-            grid=(boxes // GROUP,),
-            in_specs=[
-                pl.BlockSpec(table.shape, lambda i, n: (0, 0)),
-                pl.BlockSpec(maps.shape, lambda i, n: (0, 0, 0)),
-                pl.BlockSpec((GROUP, 128), lambda i, n: (i, 0)),
-                pl.BlockSpec(dirs.shape, lambda i, n: (0, 0)),
-                pl.BlockSpec((GROUP, 256, 128), lambda i, n: (i, 0, 0)),
-                pl.BlockSpec((GROUP, 8, 128), lambda i, n: (i, 0, 0)),
-                pl.BlockSpec((GROUP, 8, 128), lambda i, n: (i, 0, 0)),
-            ],
-            out_specs=pl.BlockSpec((3, GROUP, 128), lambda i, n: (0, i, 0)),
+            grid=(1,),
+            in_specs=whole,
+            out_specs=pl.BlockSpec((3, boxes, 128), lambda i, n: (0, 0, 0)),
             scratch_shapes=[pltpu.VMEM((maps.shape[0] * table.shape[0], 128), f32)],
         ),
         out_shape=jax.ShapeDtypeStruct((3, boxes, 128), f32),
         compiler_params=pltpu.CompilerParams(vmem_limit_bytes=48 << 20),
         name="far_velocity",
-    )(index, table, maps, down, dirs, basis, near, pq)
+    )(index, table, maps, down, freq, dirs, near, pq)
 
 
 def padded(cells, axis, width):
@@ -336,19 +301,34 @@
     h, m, l = split3_outside(waves)
     freq = jnp.concatenate([h, h, h, m, m, l], axis=1).astype(bf16)
     dirs = jnp.stack([none, none, none, charge_dirs[0], charge_dirs[1], charge_dirs[2], none, none])
-    leaf_moments, basis = leaf_moments_of(pq, freq, dirs)
+    leaf_moments = leaf_moments_of(pq, freq.T, dirs)
     nearby_moments = padded(leaf_moments, axis, boxes // 2)
-    parcel = leaf_moments[send_boxes]
-    received = lax.all_to_all(parcel, axis, split_axis=0, concat_axis=0, tiled=True)
     top_moments = upward(up_maps, upward(up_maps, leaf_moments))
-    coarse_moments = lax.all_gather(top_moments, axis, axis=0, tiled=True)
+    nodes = lax.axis_size(axis)
+    listed = leaf_moments[send_boxes.reshape(nodes, -1)]
+    tops = jnp.broadcast_to(top_moments[None], (nodes, *top_moments.shape))
+    received = lax.all_to_all(
+        jnp.concatenate([listed, tops], axis=1), axis, split_axis=0, concat_axis=0, tiled=True
+    )
+    reach = listed.shape[1]
     near = near_sums(near_source.reshape(-1), ext)
+    coarse_moments = received[:, reach:].reshape(-1, coeffs)
     coarse_locals = coarse_translate(coarse_maps, coarse_class, coarse_moments)
     leaf_down = downward(down_maps, downward(down_maps, coarse_locals))
-    table = jnp.concatenate([nearby_moments, received.reshape(-1, coeffs)], axis=0)
+    table = jnp.concatenate([nearby_moments, received[:, :reach].reshape(-1, coeffs)], axis=0)
     index = (far_class * table.shape[0] + far_source).reshape(-1)
+    maps_t = jnp.swapaxes(far_maps, 1, 2)
+    high = lax.reduce_precision(maps_t, 8, 7)
+    low = lax.reduce_precision(maps_t - high, 8, 7)
+    maps = jnp.concatenate(
+        [
+            jnp.concatenate([high, low], axis=2),
+            jnp.concatenate([high, jnp.zeros_like(low)], axis=2),
+        ],
+        axis=1,
+    ).astype(bf16)
     vel_dirs = jnp.concatenate([velocity_dirs, jnp.zeros((5, coeffs), f32)], axis=0)
-    return far_velocity_of(index, table, far_maps, leaf_down, vel_dirs, basis, near, pq)
+    return far_velocity_of(index, table, maps, leaf_down, freq, vel_dirs, near, pq)
 
 
 def solution(mesh):

time: 304 us -> 162 us (0.53)
  the two profiles are of different devices: /device:TPU:0 before, /device:TPU:12 now
where the time goes in v2:
time: 162 us; the launch traced here: 161 us
  Pallas kernels  105 us (65%)
  starting transfers between devices  19.2 us (12%)
  local copies, waits for them, and re-layouts  18.5 us (11%)
  other arithmetic  12.4 us (8%)
  matrix products  5.41 us (3%)
    pallas_call x1, Pallas kernels, far_velocity_of(): pl.pallas_call(far_kernel, grid_spec=pltpu.PrefetchScalarGridSpec(num_sca...  43.4 us
    pallas_call x1, Pallas kernels, near_sums(): pl.pallas_call(near_kernel, grid_spec=pltpu.PrefetchScalarGridSpec(num_sc...  37.7 us
    pallas_call x1, Pallas kernels, leaf_moments_of(): pl.pallas_call(moments_kernel, out_shape=jax.ShapeDtypeStruct((boxes, 128...  23.8 us
    ppermute x2, starting transfers between devices, padded(): lax.ppermute(head, axis, [(i + 1, i) for i in range(ends)])  8.95 us
    all_to_all x1, starting transfers between devices, shards(): lax.all_to_all(jnp.concatenate([listed, tops], axis=1), axis, split_axis=...  6.27 us
    another operation x2, local copies, waits for them, and re-layouts, shards(): jnp.stack([positions[0], positions[1], positions[2], charged[0], charged[...  6.22 us
    ppermute x2, starting transfers between devices, padded(): lax.ppermute(tail, axis, [(i, i + 1) for i in range(ends)])  3.95 us
    unnamed x22, local copies, waits for them, and re-layouts  3.46 us
  transfers between devices with their start and end apart: 5, of which 0 were waited for; matrix products, arithmetic and copies ran while one was open for 12% of the time, Pallas kernels for 23%

profile of v2, /device:TPU:12, one launch (start us, length us, event | category | flops | bytes accessed | tf_op | source)
XLA Modules:
  0.0 160.7 jit_solution(1366276937581256875)
XLA Ops:
  0.0 0.9 fusion.6
  1.0 2.1 %compare_convert_fusion = f32[512,1,128]{2,1,0:T(1,128)S(1)} fusion(s32[512]{0:T(512)} %param.18), kind=kLoop, calls=%fused_computation.11 | loop fusion | flops 131072 | bytes 264192 | tf_op jit(solution)/shard_map/convert_element_type | solution.py:286
  3.0 0.8 multiply_bitcast_fusion.1
  4.6 1.2 broadcast_multiply_fusion
  5.8 0.9 fusion.17
  6.7 0.9 fusion.18
  7.7 0.8 stack_broadcast_in_dim.6
  8.5 5.4 %stack.19.pq_ref = f32[512,8,128]{2,1,0:T(8,128)S(1)} concatenate(f32[512,1,128]{2,1,0:T(1,128)} %bitcast.66, f32[512,1,128]{2,1,0:T(1,128)} %bitcast.67, f32[512,1,128]{2,1,0:T(1,128)} %bitcast.65, f32[512,1,128]{2,1,0:T(1,128)} %bitcast.64, f32[512,1,128]{2,1,0:T(1,128)} %bitcast.63, f32[512,1,128]{2,1,0:T(1,128)} %bitcast.62, f32[512,1,128]{2,1,0:T(1,128)S(1)} %compare_convert_fusion, ...), dimensions={1} | concatenate | bytes 4194304 | tf_op jit(solution)/shard_map/stack | solution.py:288
  13.9 23.8 %leaf_moments.1 = f32[512,128]{1,0:T(8,128)S(1)} custom-call(f32[512,8,128]{2,1,0:T(8,128)S(1)} %stack.19.pq_ref, bf16[48,128]{1,0:T(8,128)(2,1)S(1)} %bitcast.61, f32[8,128]{1,0:T(8,128)S(1)} %pad_maximum_fusion.3.dirs_ref), custom_call_target="tpu_custom_call" | custom-call | flops 805306368 | bytes 4194304 | tf_op jit(solution)/shard_map/leaf_moments/pallas_call | solution.py:96
  40.5 6.3 %all-to-all-start = ((f32[16,16,128]{2,1,0:T(8,128)}), f32[16,16,128]{2,1,0:T(8,128)}, u32[]{:S(2)}, u32[]{:S(2)}) async-start(f32[16,16,128]{2,1,0:T(8,128)} %pad_maximum_fusion.2), calls=%async_computation | async-start | bytes 262144 | tf_op jit(solution)/shard_map/all_to_all | solution.py:310
  46.7 0.7 fusion.19
  47.5 2.0 %collective-permute-start = (f32[256,128]{1,0:T(8,128)}, f32[256,128]{1,0:T(8,128)}, u32[]{:S(2)}, u32[]{:S(2)}) collective-permute-start(f32[256,128]{1,0:T(8,128)} %get-tuple-element.15), channel_id=1, source_target_pairs={{0,1},{1,2},{2,3},{3,4},{4,5},{5,6},{6,7},{7,8},{8,9},{9,10},{10,1... | collective-permute-start | bytes 393224 | tf_op jit(solution)/shard_map/ppermute | solution.py:239
  49.5 4.4 %collective-permute-start.1 = (f32[256,128]{1,0:T(8,128)}, f32[256,128]{1,0:T(8,128)}, u32[]{:S(2)}, u32[]{:S(2)}) collective-permute-start(f32[256,128]{1,0:T(8,128)} %get-tuple-element.16), channel_id=1, source_target_pairs={{1,0},{2,1},{3,2},{4,3},{5,4},{6,5},{7,6},{8,7},{9,8},{10,9},{11,1... | collective-permute-start | bytes 393224 | tf_op jit(solution)/shard_map/ppermute | solution.py:241
  54.6 1.9 %collective-permute-start.2 = (f32[4,8,128]{2,1,0:T(8,128)}, f32[4,8,128]{2,1,0:T(8,128)S(1)}, u32[]{:S(2)}, u32[]{:S(2)}) collective-permute-start(f32[4,8,128]{2,1,0:T(8,128)} %get-tuple-element.5), channel_id=1, source_target_pairs={{0,1},{1,2},{2,3},{3,4},{4,5},{5,6},{6,7},{7,8},{8,9},{9,10},{10,1... | collective-permute-start | bytes 49160 | tf_op jit(solution)/shard_map/ppermute | solution.py:239
  56.5 4.5 %collective-permute-start.3 = (f32[4,8,128]{2,1,0:T(8,128)}, f32[4,8,128]{2,1,0:T(8,128)}, u32[]{:S(2)}, u32[]{:S(2)}) collective-permute-start(f32[4,8,128]{2,1,0:T(8,128)} %get-tuple-element.6), channel_id=1, source_target_pairs={{1,0},{2,1},{3,2},{4,3},{5,4},{6,5},{7,6},{8,7},{9,8},{10,9},{11,1... | collective-permute-start | bytes 49160 | tf_op jit(solution)/shard_map/ppermute | solution.py:241
  61.1 2.5 %copy.46 = f32[16,128,128]{1,2,0:T(8,128)} copy(f32[16,128,128]{2,1,0:T(8,128)} %param.25) | data formatting | bytes 2097152 | tf_op args[9]
  63.6 1.5 fusion.3
  65.1 0.9 multiply_add_fusion
  66.0 1.6 %fusion.1.maps_ref = bf16[16,256,256]{2,1,0:T(8,128)(2,1)} fusion(bf16[16,128,128]{2,1,0:T(8,128)(2,1)S(1)} %get-tuple-element.8, bf16[16,128,128]{2,1,0:T(8,128)(2,1)S(1)} %get-tuple-element.7), kind=kLoop, calls=%fused_computation.4 | loop fusion | flops 8388608 | bytes 3145728 | tf_op jit(solution)/shard_map/concatenate | solution.py:323
  67.7 0.9 copy.50
  68.6 1.1 reshape.112.near_ref
  69.7 0.8 copy.40
  70.5 1.1 reshape.107.index_ref
  71.6 0.7 concatenate.33.dirs_ref
  72.3 0.9 pad_maximum_fusion.ext_ref
  73.2 37.7 %near_sums.1.near_ref = f32[512,8,128]{2,1,0:T(8,128)S(1)} custom-call(s32[1024]{0:T(1024)S(1)} %reshape.112.near_ref, f32[520,8,128]{2,1,0:T(8,128)S(1)} %pad_maximum_fusion.ext_ref), custom_call_target="tpu_custom_call" | custom-call | flops 4026531840 | bytes 4194304 | tf_op jit(solution)/shard_map/near_sums/pallas_call | solution.py:149
  110.9 1.1 fusion.7
  112.0 0.9 fusion.8
  112.9 1.6 fusion.20
  115.3 0.8 slice_bitcast_fusion.2
  116.2 1.0 pad_maximum_fusion.1.table_ref
  117.2 43.4 %far_velocity.1 = f32[3,512,128]{2,1,0:T(8,128)} custom-call(s32[16384]{0:T(1024)S(1)} %reshape.107.index_ref, f32[1152,128]{1,0:T(8,128)S(1)} %pad_maximum_fusion.1.table_ref, bf16[16,256,256]{2,1,0:T(8,128)(2,1)S(1)} %copy-done.2, f32[512,128]{1,0:T(8,128)S(1)} %bitcast.60, bf16[128,48]{1,0:T(8,128)(2,1)S(1)} %copy.51.freq_ref, ...), custom_call_target="tpu_custom_call" | custom-call | tf_op jit(solution)/shard_map/far_velocity/pallas_call | solution.py:217
  (51 shorter events, 5.1 us)
Async XLA Ops:
  0.0 112.0 %copy-start = (f32[16,128,128]{2,1,0:T(8,128)S(1)}, f32[16,128,128]{2,1,0:T(8,128)}, u32[]{:S(2)}) copy-start(f32[16,128,128]{2,1,0:T(8,128)} %param.26) | copy-start | bytes 3145732
  0.0 6.7 %copy-start.5 = (f32[3,512,128]{2,1,0:T(8,128)S(1)}, f32[3,512,128]{2,1,0:T(8,128)}, u32[]{:S(2)}) copy-start(f32[3,512,128]{2,1,0:T(8,128)} %param.16) | copy-start | bytes 2359300
  4.6 3.0 %copy-start.9 = (f32[3,128]{1,0:T(4,128)S(1)}, f32[3,128]{1,0:T(4,128)}, u32[]{:S(2)}) copy-start(f32[3,128]{1,0:T(4,128)} %param.21) | copy-start | bytes 4612
  13.9 58.4 %copy-start.1 = (f32[512,8,128]{2,1,0:T(8,128)}, f32[512,8,128]{2,1,0:T(8,128)S(1)}, u32[]{:S(2)}) copy-start(f32[512,8,128]{2,1,0:T(8,128)S(1)} %stack.19.pq_ref) | copy-start | bytes 6291460
  13.9 23.8 %copy-start.3 = (f32[8,128,128]{2,1,0:T(8,128)S(1)}, f32[8,128,128]{2,1,0:T(8,128)}, u32[]{:S(2)}) copy-start(f32[8,128,128]{2,1,0:T(8,128)} %param.23) | copy-start | bytes 1572868
  13.9 25.0 %copy-start.8 = (s32[16,8]{0,1:T(8,128)S(1)}, s32[16,8]{0,1:T(8,128)}, u32[]{:S(2)}) copy-start(s32[16,8]{0,1:T(8,128)} %param.27) | copy-start | bytes 1540
  37.7 23.3 %copy-start.7 = (s32[8,128]{1,0:T(8,128)S(1)}, s32[8,128]{1,0:T(8,128)}, u32[]{:S(2)}) copy-start(s32[8,128]{1,0:T(8,128)} %param.31) | copy-start | bytes 12292
  40.5 70.4 %all-to-all-start = ((f32[16,16,128]{2,1,0:T(8,128)}), f32[16,16,128]{2,1,0:T(8,128)}, u32[]{:S(2)}, u32[]{:S(2)}) async-start(f32[16,16,128]{2,1,0:T(8,128)} %pad_maximum_fusion.2), calls=%async_computation | async-start | bytes 262144 | tf_op jit(solution)/shard_map/all_to_all | solution.py:310
  47.5 68.7 %collective-permute-start = (f32[256,128]{1,0:T(8,128)}, f32[256,128]{1,0:T(8,128)}, u32[]{:S(2)}, u32[]{:S(2)}) collective-permute-start(f32[256,128]{1,0:T(8,128)} %get-tuple-element.15), channel_id=1, source_target_pairs={{0,1},{1,2},{2,3},{3,4},{4,5},{5,6},{6,7},{7,8},{8,9},{9,10},{10,1... | collective-permute-start | bytes 393224 | tf_op jit(solution)/shard_map/ppermute | solution.py:239
  49.5 66.7 %collective-permute-start.1 = (f32[256,128]{1,0:T(8,128)}, f32[256,128]{1,0:T(8,128)}, u32[]{:S(2)}, u32[]{:S(2)}) collective-permute-start(f32[256,128]{1,0:T(8,128)} %get-tuple-element.16), channel_id=1, source_target_pairs={{1,0},{2,1},{3,2},{4,3},{5,4},{6,5},{7,6},{8,7},{9,8},{10,9},{11,1... | collective-permute-start | bytes 393224 | tf_op jit(solution)/shard_map/ppermute | solution.py:241
  54.6 17.8 %collective-permute-start.2 = (f32[4,8,128]{2,1,0:T(8,128)}, f32[4,8,128]{2,1,0:T(8,128)S(1)}, u32[]{:S(2)}, u32[]{:S(2)}) collective-permute-start(f32[4,8,128]{2,1,0:T(8,128)} %get-tuple-element.5), channel_id=1, source_target_pairs={{0,1},{1,2},{2,3},{3,4},{4,5},{5,6},{6,7},{7,8},{8,9},{9,10},{10,1... | collective-permute-start | bytes 49160 | tf_op jit(solution)/shard_map/ppermute | solution.py:239
  56.5 15.8 %collective-permute-start.3 = (f32[4,8,128]{2,1,0:T(8,128)}, f32[4,8,128]{2,1,0:T(8,128)}, u32[]{:S(2)}, u32[]{:S(2)}) collective-permute-start(f32[4,8,128]{2,1,0:T(8,128)} %get-tuple-element.6), channel_id=1, source_target_pairs={{1,0},{2,1},{3,2},{4,3},{5,4},{6,5},{7,6},{8,7},{9,8},{10,9},{11,1... | collective-permute-start | bytes 49160 | tf_op jit(solution)/shard_map/ppermute | solution.py:241
  65.1 2.6 %copy-start.6 = (s32[512,2]{0,1:T(2,128)S(1)}, s32[512,2]{0,1:T(2,128)}, u32[]{:S(2)}) copy-start(s32[512,2]{0,1:T(2,128)} %param.30) | copy-start | bytes 12292
  110.9 3.6 %copy-start.4 = (f32[8,128,128]{2,1,0:T(8,128)S(1)}, f32[8,128,128]{2,1,0:T(8,128)}, u32[]{:S(2)}) copy-start(f32[8,128,128]{2,1,0:T(8,128)} %param.24) | copy-start | bytes 1572868
  112.0 5.2 %copy-start.2 = (bf16[16,256,256]{2,1,0:T(8,128)(2,1)S(1)}, bf16[16,256,256]{2,1,0:T(8,128)(2,1)}, u32[]{:S(2)}) copy-start(bf16[16,256,256]{2,1,0:T(8,128)(2,1)} %fusion.1.maps_ref) | copy-start | bytes 6291460

commit v3 on v2

--- a/solution.py
+++ b/solution.py
@@ -52,10 +52,6 @@
     return h, m, lax.reduce_precision(x - h - m, 8, 7)
 
 
-def nt(a, b):
-    return lax.dot_general(a, b, (((1,), (1,)), ((), ())), preferred_element_type=f32)
-
-
 def tn(a, b):
     return lax.dot_general(a, b, (((0,), (0,)), ((), ())), preferred_element_type=f32)
 
@@ -81,27 +77,41 @@
     return pieces(out)
 
 
-def moments_kernel(pq_ref, freq_ref, dirs_ref, moment_ref):
+def moments_kernel(counts_ref, pos_ref, str_ref, freq_ref, dirs_ref, moment_ref, pq_ref):
+    lane = lax.broadcasted_iota(jnp.int32, (1, 128), 1)
+    one = jnp.ones((1, 128), f32)
+
     def box(b, _):
-        angles, charges = stacks_of(pq_ref[b])
+        keep = jnp.where(lane < counts_ref[b], 1.0, 0.0)
+        coords = [pos_ref[i, pl.ds(b, 1), :] for i in range(3)]
+        charged = [str_ref[i, pl.ds(b, 1), :] * keep for i in range(3)]
+        tile = jnp.concatenate(coords + charged + [keep, one], axis=0)
+        pq_ref[b] = tile
+        angles, charges = stacks_of(tile)
         got = split_product(charges, cos_turns(tn(angles, freq_ref[...])))
         moment_ref[pl.ds(b, 1), :] = jnp.sum(got * dirs_ref[...], axis=0, keepdims=True)
         return 0
 
-    lax.fori_loop(0, pq_ref.shape[0], box, 0, unroll=32)
-
-
-def leaf_moments_of(pq, freq, dirs):
-    boxes = pq.shape[0]
+    lax.fori_loop(0, pq_ref.shape[0], box, 0, unroll=64)
+
+
+def leaf_moments_of(counts, positions, strengths, freq, dirs):
+    boxes = counts.shape[0]
+    vmem = pl.BlockSpec(memory_space=pltpu.VMEM)
     return pl.pallas_call(
         moments_kernel,
-        out_shape=jax.ShapeDtypeStruct((boxes, 128), f32),
+        in_specs=[pl.BlockSpec(memory_space=pltpu.SMEM), vmem, vmem, vmem, vmem],
+        out_specs=[vmem, vmem],
+        out_shape=[
+            jax.ShapeDtypeStruct((boxes, 128), f32),
+            jax.ShapeDtypeStruct((boxes, ROWS, 128), f32),
+        ],
         compiler_params=pltpu.CompilerParams(vmem_limit_bytes=32 << 20),
         cost_estimate=pl.CostEstimate(
             flops=boxes * 128 * 128 * 96, bytes_accessed=boxes * 8192, transcendentals=0
         ),
         name="leaf_moments",
-    )(pq, freq, dirs)
+    )(counts, positions, strengths, freq, dirs)
 
 
 def near_kernel(near_ref, ext_ref, out_ref, source_ref, target_ref, charge_ref):
@@ -140,7 +150,7 @@
         out_ref[b] = split_product(charges, inv * inv * inv)
         return 0
 
-    lax.fori_loop(0, out_ref.shape[0], box, 0, unroll=32)
+    lax.fori_loop(0, out_ref.shape[0], box, 0, unroll=64)
 
 
 def near_sums(near_rows, ext):
@@ -205,7 +215,7 @@
             out_ref[i, pl.ds(b, 1), :] = (far[i : i + 1] + value * inverse_four_pi) * keep
         return 0
 
-    lax.fori_loop(0, boxes, box, 0, unroll=16)
+    lax.fori_loop(0, boxes, box, 0, unroll=32)
 
 
 def far_velocity_of(index, table, maps, down, freq, dirs, near, pq):
@@ -229,18 +239,20 @@
     )(index, table, maps, down, freq, dirs, near, pq)
 
 
-def padded(cells, axis, width):
+def reached(moments, tiles, axis, width):
     count = lax.axis_size(axis)
     ends = count - 1
-    head = cells[:width]
-    tail = cells[cells.shape[0] - width :]
-    return jnp.concatenate(
-        [
-            lax.ppermute(tail, axis, [(i, i + 1) for i in range(ends)]),
-            cells,
-            lax.ppermute(head, axis, [(i + 1, i) for i in range(ends)]),
-        ],
-        axis=0,
+    total = moments.shape[0]
+    head = jnp.concatenate([moments[:width], tiles[:HW].reshape(HW * ROWS, -1)], axis=0)
+    tail = jnp.concatenate(
+        [moments[total - width :], tiles[total - HW :].reshape(HW * ROWS, -1)], axis=0
+    )
+    before = lax.ppermute(tail, axis, [(i, i + 1) for i in range(ends)])
+    after = lax.ppermute(head, axis, [(i + 1, i) for i in range(ends)])
+    near_tiles = [part[width:].reshape(HW, ROWS, -1) for part in (before, after)]
+    return (
+        [before[:width], moments, after[:width]],
+        jnp.concatenate([near_tiles[0], tiles, near_tiles[1]], axis=0),
     )
 
 
@@ -280,17 +292,8 @@
     coarse_class,
 ):
     axis = ("curve", "sub")
-    boxes, slots = positions.shape[1:]
+    boxes = positions.shape[1]
     coeffs = frequencies.shape[1]
-    slot_index = jnp.arange(slots, dtype=jnp.int32)
-    occupied = (slot_index[None, :] < counts[:, None]).astype(f32)
-    charged = strengths * occupied[None]
-    pq = jnp.stack(
-        [positions[0], positions[1], positions[2], charged[0], charged[1], charged[2], occupied,
-         jnp.ones_like(occupied)],
-        axis=1,
-    )
-    ext = padded(pq, axis, HW)
     none = jnp.zeros((coeffs,), f32)
     turn = 1.0 / (2.0 * math.pi)
     waves = jnp.stack(
@@ -301,8 +304,8 @@
     h, m, l = split3_outside(waves)
     freq = jnp.concatenate([h, h, h, m, m, l], axis=1).astype(bf16)
     dirs = jnp.stack([none, none, none, charge_dirs[0], charge_dirs[1], charge_dirs[2], none, none])
-    leaf_moments = leaf_moments_of(pq, freq.T, dirs)
-    nearby_moments = padded(leaf_moments, axis, boxes // 2)
+    leaf_moments, pq = leaf_moments_of(counts, positions, strengths, freq.T, dirs)
+    nearby_moments, ext = reached(leaf_moments, pq, axis, boxes // 2)
     top_moments = upward(up_maps, upward(up_maps, leaf_moments))
     nodes = lax.axis_size(axis)
     listed = leaf_moments[send_boxes.reshape(nodes, -1)]
@@ -315,7 +318,7 @@
     coarse_moments = received[:, reach:].reshape(-1, coeffs)
     coarse_locals = coarse_translate(coarse_maps, coarse_class, coarse_moments)
     leaf_down = downward(down_maps, downward(down_maps, coarse_locals))
-    table = jnp.concatenate([nearby_moments, received[:, :reach].reshape(-1, coeffs)], axis=0)
+    table = jnp.concatenate([*nearby_moments, received[:, :reach].reshape(-1, coeffs)], axis=0)
     index = (far_class * table.shape[0] + far_source).reshape(-1)
     maps_t = jnp.swapaxes(far_maps, 1, 2)
     high = lax.reduce_precision(maps_t, 8, 7)

time: 162 us -> 144 us (0.89)
  the two profiles are of different devices: /device:TPU:12 before, /device:TPU:0 now
where the time goes in v3:
time: 144 us; the launch traced here: 143 us
  Pallas kernels  97.6 us (68%)
  local copies, waits for them, and re-layouts  16 us (11%)
  starting transfers between devices  13 us (9%)
  other arithmetic  10.8 us (8%)
  matrix products  5.42 us (4%)
    pallas_call x1, Pallas kernels, far_velocity_of(): pl.pallas_call(far_kernel, grid_spec=pltpu.PrefetchScalarGridSpec(num_sca...  39.6 us
    pallas_call x1, Pallas kernels, near_sums(): pl.pallas_call(near_kernel, grid_spec=pltpu.PrefetchScalarGridSpec(num_sc...  35 us
    pallas_call x1, Pallas kernels, leaf_moments_of(): pl.pallas_call(moments_kernel, in_specs=[pl.BlockSpec(memory_space=pltpu....  23 us
    all_to_all x1, starting transfers between devices, shards(): lax.all_to_all(jnp.concatenate([listed, tops], axis=1), axis, split_axis=...  8.67 us
    unnamed x30, local copies, waits for them, and re-layouts  6.41 us
    ppermute x1, starting transfers between devices, reached(): before = lax.ppermute(tail, axis, [(i, i + 1) for i in range(ends)])  3.02 us
    concatenate x1, other arithmetic, shards(): jnp.concatenate([jnp.concatenate([high, low], axis=2), jnp.concatenate([h...  2.95 us
  transfers between devices with their start and end apart: 3, of which 0 were waited for; matrix products, arithmetic and copies ran while one was open for 15% of the time, Pallas kernels for 24%

profile of v3, /device:TPU:0, one launch (start us, length us, event | category | flops | bytes accessed | tf_op | source)
XLA Modules:
  0.0 143.2 jit_solution(13944428512396102221)
XLA Ops:
  0.0 0.8 multiply_bitcast_fusion.1
  1.6 0.8 pad_maximum_fusion.5.dirs_ref
  2.3 1.1 copy-done.3
  3.5 1.1 copy-done.4
  4.6 0.7 copy-done.5
  5.3 23.0 %leaf_moments.1 = (f32[512,128]{1,0:T(8,128)S(1)}, f32[512,8,128]{2,1,0:T(8,128)S(1)}) custom-call(s32[512]{0:T(512)S(1)} %copy-done.5, f32[3,512,128]{2,1,0:T(8,128)S(1)} %copy-done.3, f32[3,512,128]{2,1,0:T(8,128)S(1)} %copy-done.4, bf16[48,128]{1,0:T(8,128)(2,1)S(1)} %bitcast.59, f32[8,128]{1,0:T(8,128)S(1)} %pad_maximum_fusion.5.dirs_ref), custom_call_target="tpu_custom_call" | custom-call | flops 805306368 | bytes 4194304 | tf_op jit(solution)/shard_map/leaf_moments/pallas_call | solution.py:101
  28.4 0.7 pad_maximum_fusion.2
  29.1 3.0 %collective-permute-start = (f32[288,128]{1,0:T(8,128)}, f32[288,128]{1,0:T(8,128)}, u32[]{:S(2)}, u32[]{:S(2)}) collective-permute-start(f32[288,128]{1,0:T(8,128)} %pad_maximum_fusion.2), channel_id=1, source_target_pairs={{0,1},{1,2},{2,3},{3,4},{4,5},{5,6},{6,7},{7,8},{8,9},{9,10},{10,1... | collective-permute-start | bytes 442376 | tf_op jit(solution)/shard_map/ppermute | solution.py:250
  32.1 0.7 pad_maximum_fusion.3
  32.8 1.3 collective-permute-start.1
  34.1 0.7 convolution_bitcast_fusion
  36.1 0.7 pad_maximum_fusion.4
  36.8 8.7 %all-to-all-start = ((f32[16,16,128]{2,1,0:T(8,128)}), f32[16,16,128]{2,1,0:T(8,128)}, u32[]{:S(2)}, u32[]{:S(2)}) async-start(f32[16,16,128]{2,1,0:T(8,128)} %pad_maximum_fusion.4), calls=%async_computation | async-start | bytes 262144 | tf_op jit(solution)/shard_map/all_to_all | solution.py:313
  45.6 0.9 copy.44
  46.4 1.1 reshape.79.near_ref
  47.6 2.5 %copy.40 = f32[16,128,128]{1,2,0:T(8,128)} copy(f32[16,128,128]{2,1,0:T(8,128)} %param.25) | data formatting | bytes 2097152 | tf_op args[9]
  50.2 2.5 %fusion.3 = (bf16[16,128,128]{2,1,0:T(8,128)(2,1)}, bf16[16,128,128]{2,1,0:T(8,128)(2,1)}) fusion(f32[16,128,128]{1,2,0:T(8,128)} %copy.40), kind=kLoop, calls=%fused_computation.10 | loop fusion | flops 1310720 | bytes 2097152 | tf_op jit(solution)/shard_map/convert.5
  52.6 0.9 multiply_add_fusion
  53.5 0.8 copy.36
  54.3 1.1 reshape.72.index_ref
  55.4 2.9 %fusion.1.maps_ref = bf16[16,256,256]{2,1,0:T(8,128)(2,1)} fusion(bf16[16,128,128]{2,1,0:T(8,128)(2,1)} %get-tuple-element.12, bf16[16,128,128]{2,1,0:T(8,128)(2,1)} %get-tuple-element.11), kind=kLoop, calls=%fused_computation.4 | loop fusion | flops 8388608 | bytes 3145728 | tf_op jit(solution)/shard_map/concatenate | solution.py:326
  58.4 0.7 slice_bitcast_fusion.4
  59.1 0.7 slice_bitcast_fusion.3
  60.0 1.6 %slice.58 = f32[256,128]{1,0:T(8,128)} slice(f32[288,128]{1,0:T(8,128)} %collective-permute-done), slice={[0:256], [0:128]} | slice | bytes 262144 | tf_op jit(solution)/shard_map/slice | solution.py:254
  61.6 1.6 %slice.59 = f32[256,128]{1,0:T(8,128)} slice(f32[288,128]{1,0:T(8,128)} %collective-permute-done.1), slice={[0:256], [0:128]} | slice | bytes 262144 | tf_op jit(solution)/shard_map/slice | solution.py:254
  63.1 35.0 %near_sums.1.near_ref = f32[512,8,128]{2,1,0:T(8,128)S(1)} custom-call(s32[1024]{0:T(1024)S(1)} %reshape.79.near_ref, f32[520,8,128]{2,1,0:T(8,128)S(1)} %pad_maximum_fusion.ext_ref), custom_call_target="tpu_custom_call" | custom-call | flops 4026531840 | bytes 4194304 | tf_op jit(solution)/shard_map/near_sums/pallas_call | solution.py:159
  98.2 1.1 fusion.6
  99.3 0.9 fusion.7
  100.2 1.6 %fusion.16 = f32[8,8,128]{2,0,1:T(8,128)S(1)} fusion(f32[8,128,1]{1,0,2:T(8,128)S(1)} %fusion.7, f32[8,128,128]{2,1,0:T(8,128)} %param.24), kind=kOutput, calls=%fused_computation.53 | convolution fusion | flops 12582912 | bytes 561152 | tf_op jit(solution)/shard_map/jkl,ql->qjk/dot_general | solution.py:265
  101.8 0.7 fusion.9
  102.7 0.8 slice_bitcast_fusion.2
  103.6 39.6 %far_velocity.1 = f32[3,512,128]{2,1,0:T(8,128)} custom-call(s32[16384]{0:T(1024)S(1)} %reshape.72.index_ref, f32[1152,128]{1,0:T(8,128)S(1)} %pad_maximum_fusion.1.table_ref, bf16[16,256,256]{2,1,0:T(8,128)(2,1)S(1)} %copy-done.2, f32[512,128]{1,0:T(8,128)S(1)} %bitcast.58, bf16[128,48]{1,0:T(8,128)(2,1)S(1)} %copy.45.freq_ref, ...), custom_call_target="tpu_custom_call" | custom-call | tf_op jit(solution)/shard_map/far_velocity/pallas_call | solution.py:227
  (54 shorter events, 2.7 us)
Async XLA Ops:
  0.0 99.3 %copy-start = (f32[16,128,128]{2,1,0:T(8,128)S(1)}, f32[16,128,128]{2,1,0:T(8,128)}, u32[]{:S(2)}) copy-start(f32[16,128,128]{2,1,0:T(8,128)} %param.26) | copy-start | bytes 3145732
  2.3 1.1 copy-start.3
  3.5 1.1 copy-start.4
  4.6 0.7 copy-start.5
  5.3 28.8 %copy-start.6 = (f32[8,128,128]{2,1,0:T(8,128)S(1)}, f32[8,128,128]{2,1,0:T(8,128)}, u32[]{:S(2)}) copy-start(f32[8,128,128]{2,1,0:T(8,128)} %param.23) | copy-start | bytes 1572868
  5.3 29.9 %copy-start.12 = (s32[16,8]{0,1:T(8,128)S(1)}, s32[16,8]{0,1:T(8,128)}, u32[]{:S(2)}) copy-start(s32[16,8]{0,1:T(8,128)} %param.27) | copy-start | bytes 1540
  28.3 31.5 %copy-start.1 = (f32[512,8,128]{2,1,0:T(8,128)}, f32[512,8,128]{2,1,0:T(8,128)S(1)}, u32[]{:S(2)}) copy-start(f32[512,8,128]{2,1,0:T(8,128)S(1)} %get-tuple-element.8.pq_ref) | copy-start | bytes 6291460
  28.3 17.3 %copy-start.10 = (s32[512,2]{0,1:T(2,128)S(1)}, s32[512,2]{0,1:T(2,128)}, u32[]{:S(2)}) copy-start(s32[512,2]{0,1:T(2,128)} %param.30) | copy-start | bytes 12292
  28.3 19.2 %copy-start.11 = (s32[8,128]{1,0:T(8,128)S(1)}, s32[8,128]{1,0:T(8,128)}, u32[]{:S(2)}) copy-start(s32[8,128]{1,0:T(8,128)} %param.31) | copy-start | bytes 12292
  29.1 29.3 %collective-permute-start = (f32[288,128]{1,0:T(8,128)}, f32[288,128]{1,0:T(8,128)}, u32[]{:S(2)}, u32[]{:S(2)}) collective-permute-start(f32[288,128]{1,0:T(8,128)} %pad_maximum_fusion.2), channel_id=1, source_target_pairs={{0,1},{1,2},{2,3},{3,4},{4,5},{5,6},{6,7},{7,8},{8,9},{9,10},{10,1... | collective-permute-start | bytes 442376 | tf_op jit(solution)/shard_map/ppermute | solution.py:250
  32.8 26.3 %collective-permute-start.1 = (f32[288,128]{1,0:T(8,128)}, f32[288,128]{1,0:T(8,128)}, u32[]{:S(2)}, u32[]{:S(2)}) collective-permute-start(f32[288,128]{1,0:T(8,128)} %pad_maximum_fusion.3), channel_id=1, source_target_pairs={{1,0},{2,1},{3,2},{4,3},{5,4},{6,5},{7,6},{8,7},{9,8},{10,9},{11,1... | collective-permute-start | bytes 442376 | tf_op jit(solution)/shard_map/ppermute | solution.py:251
  36.8 61.4 %all-to-all-start = ((f32[16,16,128]{2,1,0:T(8,128)}), f32[16,16,128]{2,1,0:T(8,128)}, u32[]{:S(2)}, u32[]{:S(2)}) async-start(f32[16,16,128]{2,1,0:T(8,128)} %pad_maximum_fusion.4), calls=%async_computation | async-start | bytes 262144 | tf_op jit(solution)/shard_map/all_to_all | solution.py:313
  47.6 7.8 %copy-start.13 = (f32[3,128]{1,0:T(4,128)S(1)}, f32[3,128]{1,0:T(4,128)}, u32[]{:S(2)}) copy-start(f32[3,128]{1,0:T(4,128)} %param.22) | copy-start | bytes 4612
  98.2 3.6 %copy-start.7 = (f32[8,128,128]{2,1,0:T(8,128)S(1)}, f32[8,128,128]{2,1,0:T(8,128)}, u32[]{:S(2)}) copy-start(f32[8,128,128]{2,1,0:T(8,128)} %param.24) | copy-start | bytes 1572868
  98.2 5.3 %copy-start.8 = (f32[256,128]{1,0:T(8,128)S(1)}, f32[256,128]{1,0:T(8,128)}, u32[]{:S(2)}) copy-start(f32[256,128]{1,0:T(8,128)} %slice.58) | copy-start | bytes 393220
  98.2 5.3 %copy-start.9 = (f32[256,128]{1,0:T(8,128)S(1)}, f32[256,128]{1,0:T(8,128)}, u32[]{:S(2)}) copy-start(f32[256,128]{1,0:T(8,128)} %slice.59) | copy-start | bytes 393220
  99.3 4.3 %copy-start.2 = (bf16[16,256,256]{2,1,0:T(8,128)(2,1)S(1)}, bf16[16,256,256]{2,1,0:T(8,128)(2,1)}, u32[]{:S(2)}) copy-start(bf16[16,256,256]{2,1,0:T(8,128)(2,1)} %fusion.1.maps_ref) | copy-start | bytes 6291460
